TPU v7x, 128 devices: a whole 4x4x4 slice. The times are simulated.
128 devices in a mesh: frow: 8 (over z, core), fcol: 8 (over y_hi, x), chan: 2 (over y_lo).
Axes of the slice: x: 4, y: 4 (y_hi: 2, y_lo: 2; y = y_hi * 2 + y_lo), z: 4, core: 2. Of those that a mesh axis runs over, the one named last changes fastest.
Arguments:
- image_cube: float32 [32, 512, 2048], P('chan', 'frow', 'fcol'), may hold values from -40 to 40
- weights: float32 [3, 512, 2048], P(None, 'frow', 'fcol'), may hold values from 0.5 to 2
Outputs:
- backprojected: float32 [32, 512, 2048], P('chan', 'frow', 'fcol')
- lowrank: float32 [32, 512, 2048], P('chan', 'frow', 'fcol')
All inputs are finite; a program needn't handle non-finite values.
Results may differ from a plain program's by a relative error of at most 0.0003.
Values sent between devices are 32-bit elements; how exact they have to be, the bound alone decides.
No kernel may reach another device: no remote copies, remote signals or barrier semaphores. Data moves between devices by JAX's collectives and lax.ppermute only.
A program may use at most 128 MiB of HBM per device.

v0:
```python
import math

import jax
import jax.numpy as jnp
import numpy as np
from jax import lax
from jax.sharding import PartitionSpec as P

JSWEEPS = 3


filter_taps = (0.0625, 0.25, 0.375, 0.25, 0.0625)
band_levels = (12.0, 4.0, 2.5)
rank_level = 2.0
tiny_value = 1e-30


def padded(x, sides, width):
    for axis, dim in sides:
        peers, length = (lax.axis_size(axis), x.shape[dim])
        up = [(i, (i + 1) % peers) for i in range(peers - 1)]
        down = [(j, i) for i, j in up]
        last = lax.slice_in_dim(x, length - width, length, axis=dim)
        leading = lax.slice_in_dim(x, 0, width, axis=dim)
        before = lax.ppermute(last, axis, up)
        after = lax.ppermute(leading, axis, down)
        x = jnp.concatenate([before, x, after], axis=dim)
    return x


def smooth(extended, dilation):
    reach_cells = 2 * dilation
    row_count = extended.shape[-2] - 2 * reach_cells
    col_count = extended.shape[-1] - 2 * reach_cells
    across = filter_taps[0] * extended[..., 0:row_count, :]
    for tap_index in range(1, 5):
        offset = tap_index * dilation
        across = across + filter_taps[tap_index] * extended[..., offset : offset + row_count, :]
    result = filter_taps[0] * across[..., 0:col_count]
    for tap_index in range(1, 5):
        offset = tap_index * dilation
        result = result + filter_taps[tap_index] * across[..., offset : offset + col_count]
    return result


def tournament(order_size):
    players = list(range(order_size))
    tables = []
    for round_index in range(order_size - 1):
        first_list = []
        second_list = []
        for slot_index in range(order_size // 2):
            left_one = players[slot_index]
            right_one = players[order_size - 1 - slot_index]
            first_list.append(min(left_one, right_one))
            second_list.append(max(left_one, right_one))
        order_list = np.array(first_list + second_list, np.int32)
        inverse_list = np.argsort(order_list).astype(np.int32)
        tables.append(
            (
                np.array(first_list, np.int32),
                np.array(second_list, np.int32),
                order_list,
                inverse_list,
            )
        )
        players = [players[0], players[-1]] + players[1:-1]
    return tables


def jacobi(gram_matrix):
    order_size = gram_matrix.shape[0]
    half_size = order_size // 2
    tables = tournament(order_size)
    identity_matrix = jnp.eye(order_size, dtype=gram_matrix.dtype)

    def one_round(matrix, vectors, first_list, second_list, order_list, inverse_list):
        diag_values = jnp.diagonal(matrix)
        left_diag = diag_values[first_list]
        right_diag = diag_values[second_list]
        cross_term = matrix[first_list, second_list]
        gap_value = right_diag - left_diag
        sign_part = jnp.where(gap_value >= 0, 1.0, -1.0)
        tangent = (
            sign_part
            * 2.0
            * cross_term
            / (
                jnp.abs(gap_value)
                + jnp.sqrt(gap_value * gap_value + 4.0 * cross_term * cross_term)
                + tiny_value
            )
        )
        cosine = 1.0 / jnp.sqrt(1.0 + tangent * tangent)
        sine_part = tangent * cosine

        def turn_columns(block):
            placed = block[:, order_list]
            left_cols = placed[:, :half_size]
            right_cols = placed[:, half_size:]
            turned = jnp.concatenate(
                [
                    cosine * left_cols - sine_part * right_cols,
                    sine_part * left_cols + cosine * right_cols,
                ],
                axis=1,
            )
            return turned[:, inverse_list]

        matrix = turn_columns(matrix)
        matrix = turn_columns(matrix.T).T
        vectors = turn_columns(vectors)
        return (matrix, vectors)

    def sweep(counter, carried):
        matrix, vectors = carried
        for first_list, second_list, order_list, inverse_list in tables:
            matrix, vectors = one_round(
                matrix, vectors, first_list, second_list, order_list, inverse_list
            )
        return (matrix, vectors)

    matrix, vectors = lax.fori_loop(0, JSWEEPS, sweep, (gram_matrix, identity_matrix))
    return (jnp.diagonal(matrix), vectors)


def spectral_map(gram_matrix, threshold):
    values, vectors = jacobi(gram_matrix)
    factors = 1.0 - threshold / jnp.sqrt(jnp.maximum(values, threshold * threshold))
    return jnp.dot(vectors * factors[None, :], vectors.T, precision=lax.Precision.HIGHEST)


def shards(image_cube, weights):
    local_channels, row_count, col_count = image_cube.shape
    highest = lax.Precision.HIGHEST
    coarse_one = smooth(padded(image_cube, (("frow", 1), ("fcol", 2)), 2), 1)
    coarse_two = smooth(padded(coarse_one, (("frow", 1), ("fcol", 2)), 4), 2)
    band_list = (image_cube - coarse_one, coarse_one - coarse_two, coarse_two)
    squares = jnp.stack([jnp.sum(band * band, axis=0) for band in band_list])
    totals = lax.psum(squares, "chan")
    levels = jnp.asarray(band_levels, jnp.float32)[:, None, None] * weights
    factors = levels / jnp.sqrt(jnp.maximum(totals, levels * levels))
    dual_list = [band_list[band_index] * factors[band_index] for band_index in range(3)]
    inner_part = smooth(padded(dual_list[2] - dual_list[1], (("frow", 1), ("fcol", 2)), 4), 2)
    summed = dual_list[1] - dual_list[0] + inner_part
    backprojected = dual_list[0] + smooth(padded(summed, (("frow", 1), ("fcol", 2)), 2), 1)
    pixels = row_count * col_count
    threshold = rank_level * math.sqrt(pixels)
    flat_cube = image_cube.reshape(local_channels, pixels)
    gathered = lax.all_gather(flat_cube, "chan", axis=0, tiled=True)
    mixing = spectral_map(jnp.dot(gathered, gathered.T, precision=highest), threshold)
    own_rows = lax.dynamic_slice_in_dim(
        mixing, lax.axis_index("chan") * local_channels, local_channels, 0
    )
    lowrank = jnp.dot(own_rows, gathered, precision=highest)
    return (backprojected, lowrank.reshape(image_cube.shape))


def solution(mesh):
    placed = (P("chan", "frow", "fcol"), P(None, "frow", "fcol"))
    return jax.shard_map(
        shards,
        mesh=mesh,
        in_specs=placed,
        out_specs=(P("chan", "frow", "fcol"), P("chan", "frow", "fcol")),
        check_vma=False,
    )
```

profile of v0, /device:TPU:7, one launch (start us, length us, event | category | flops | bytes accessed | tf_op | source)
XLA Modules:
  0.0 831.6 jit_solution(13520806871725487908)
XLA Ops:
  8.2 4.1 collective-permute-start
  22.7 4.9 collective-permute-start.2
  29.6 6.2 collective-permute-done.3
  41.3 2.7 fusion.233
  46.5 5.1 collective-permute-start.4
  51.6 2.5 copy.703
  65.3 3.6 collective-permute-start.7
  68.9 4.7 collective-permute-done.7
  82.2 31.3 %all-reduce.2.cloned.1.call-done = f32[3,64,256]{1,2,0:T(8,128)} async-done(((f32[3,64,256]{1,2,0:T(8,128)}), f32[3,64,256]{1,2,0:T(8,128)}) %all-reduce.2.cloned.1.call-update) | async-done | bytes 196624 | tf_op jit(solution)/shard_map/psum | solution.py:140
  114.7 2.8 multiply_subtract_fusion.93
  117.4 2.6 fusion.232
  122.6 3.7 collective-permute-start.8
  126.3 2.5 copy.707
  137.8 4.3 collective-permute-start.10
  146.1 4.3 collective-permute-done.11
  150.5 3.4 pad_maximum_fusion.94
  157.0 2.7 fusion.231
  162.2 4.3 collective-permute-start.12
  179.9 3.5 collective-permute-start.15
  184.0 4.0 collective-permute-done.15
  188.0 3.4 pad_maximum_fusion.96
  195.7 3.5 copy.714
  199.5 4.1 fusion.235
  203.8 617.1 %while.15 = (s32[]{:T(128)}, f32[32,32]{1,0:T(8,128)S(1)}, f32[32,32]{0,1:T(8,128)S(1)}, s32[]{:T(128)}, s32[32]{0:T(128)S(1)}, /*index=5*/s32[16]{0:T(128)S(1)}...) while((s32[]{:T(128)}, f32[32,32]{1,0:T(8,128)S(1)}, ...), condition=%wide.region_5.6_spmd.clone.clone.clone, body=%wide.region_4.5_spmd.sunk.clone.clone.clone.sunk | while | flops 513938 | bytes 4194541 | solution.py:123
  (3048 shorter events, 692.5 us)
Async XLA Ops:
  7.2 106.3 %all-reduce.2.cloned.1.call-start = ((), (), s32[]{:S(2)}) async-start(), calls=%async_computation | async-start | bytes 786432 | tf_op jit(solution)/shard_map/psum | solution.py:140
  8.2 8.6 %collective-permute-start = (f32[16,2,256]{2,0,1:T(8,128)S(1)}, f32[16,2,256]{2,0,1:T(8,128)S(1)}, u32[]{:S(2)}, u32[]{:S(2)}) collective-permute-start(f32[16,2,256]{2,0,1:T(8,128)S(1)} %copy.715), channel_id=1, source_target_pairs={{0,16},{16,32},{32,48},{48,64},{64,80},{80,96},{96,112},{1,17},{17... | collective-permute-start | bytes 98312 | tf_op jit(solution)/shard_map/ppermute | solution.py:25
  12.3 6.9 collective-permute-start.1
  16.8 18.9 %copy-start = (f32[16,64,256]{1,0,2:T(8,128)}, f32[16,64,256]{1,0,2:T(8,128)S(1)}, u32[]{:S(2)}) copy-start(f32[16,64,256]{1,0,2:T(8,128)S(1)} %copy.700) | copy-start | bytes 3145732
  21.7 14.0 %copy-start.3 = (f32[16,2,256]{1,0,2:T(8,128)S(1)}, f32[16,2,256]{1,0,2:T(8,128)}, u32[]{:S(2)}) copy-start(f32[16,2,256]{1,0,2:T(8,128)} %copy.697) | copy-start | bytes 98308
  21.7 14.0 %copy-start.5 = (f32[16,2,256]{1,0,2:T(8,128)S(1)}, f32[16,2,256]{1,0,2:T(8,128)}, u32[]{:S(2)}) copy-start(f32[16,2,256]{1,0,2:T(8,128)} %copy.699) | copy-start | bytes 98308
  22.7 6.8 collective-permute-start.2
  27.6 8.1 collective-permute-start.3
  46.5 9.5 %collective-permute-start.4 = (f32[16,4,256]{2,0,1:T(8,128)S(1)}, f32[16,4,256]{2,0,1:T(8,128)S(1)}, u32[]{:S(2)}, u32[]{:S(2)}) collective-permute-start(f32[16,4,256]{2,0,1:T(8,128)S(1)} %copy.702), channel_id=1, source_target_pairs={{0,16},{16,32},{32,48},{48,64},{64,80},{80,96},{96,112},{1,17},{17... | collective-permute-start | bytes 196616 | tf_op jit(solution)/shard_map/ppermute | solution.py:25
  54.1 5.6 collective-permute-start.5
  63.2 5.6 collective-permute-start.6
  65.3 8.3 collective-permute-start.7
  79.3 34.2 %copy-start.164 = (f32[3]{0:T(128)S(1)}, f32[3]{0:T(128)}, u32[]{:S(2)}) copy-start(f32[3]{0:T(128)} %constant.366.clone) | copy-start | bytes 40
  82.0 117.5 %all-gather.2.cloned.1.call-start = ((), (), s32[]{:S(2)}) async-start(), calls=%async_computation.1 | async-start | bytes 3145728 | tf_op jit(solution)/shard_map/all_gather | solution.py:150
  122.6 8.2 collective-permute-start.8
  128.8 5.6 collective-permute-start.9
  137.8 8.3 collective-permute-start.10
  142.2 8.3 collective-permute-start.11
  162.2 8.8 %collective-permute-start.12 = (f32[16,2,256]{2,0,1:T(8,128)S(1)}, f32[16,2,256]{2,0,1:T(8,128)S(1)}, u32[]{:S(2)}, u32[]{:S(2)}) collective-permute-start(f32[16,2,256]{2,0,1:T(8,128)S(1)} %copy.710), channel_id=1, source_target_pairs={{0,16},{16,32},{32,48},{48,64},{64,80},{80,96},{96,112},{1,17},{17... | collective-permute-start | bytes 98312 | tf_op jit(solution)/shard_map/ppermute | solution.py:25
  169.1 5.6 collective-permute-start.13
  178.0 6.0 collective-permute-start.14
  179.9 8.1 collective-permute-start.15
  203.8 617.1 %copy-start.42 = (s32[32]{0:T(128)S(1)}, s32[32]{0:T(128)}, u32[]{:S(2)}) copy-start(s32[32]{0:T(128)} %or_bitcast_fusion.1) | copy-start | bytes 388
  203.8 618.1 %copy-start.2 = (f32[32,16384]{1,0:T(8,128)S(1)}, f32[32,16384]{1,0:T(8,128)}, u32[]{:S(2)}) copy-start(f32[32,16384]{1,0:T(8,128)} %all-gather.2.cloned.1.call-done) | copy-start | bytes 6291460
  (416 other events, 3325.6 us)
Sparse Core Ops, SparseCore 0:
  82.1 31.3 all-reduce.1
  146.3 36.0 all-gather.1
where the time goes:
time: 840 us; the launch traced here: 832 us
  local copies, waits for them, and re-layouts  642 us (76%)
  other arithmetic  55.7 us (7%)
  waiting for transfers between devices  54.2 us (6%)
  starting transfers between devices  49.5 us (6%)
  between operations  15.2 us (2%)
  loops' own time  9.77 us (1%)
    gather x462, local copies, waits for them, and re-layouts, turn_columns(): return turned[:, inverse_list]  173 us
    gather x279, local copies, waits for them, and re-layouts, turn_columns(): placed = block[:, order_list]  160 us
    gather x93, local copies, waits for them, and re-layouts, one_round(): diag_values = jnp.diagonal(matrix)  66.6 us
    gather x93, local copies, waits for them, and re-layouts, one_round(): cross_term = matrix[first_list, second_list]  61.6 us
    gather x93, local copies, waits for them, and re-layouts, one_round(): left_diag = diag_values[first_list]  61.2 us
    gather x93, local copies, waits for them, and re-layouts, one_round(): right_diag = diag_values[second_list]  61.1 us
    psum x1, waiting for transfers between devices, shards(): totals = lax.psum(squares, 'chan')  31.3 us
    ppermute x8, starting transfers between devices, padded(): before = lax.ppermute(last, axis, up)  30.4 us
  transfers between devices with their start and end apart: 18, of which 8 were waited for; matrix products, arithmetic and copies ran while one was open for 6% of the time, Pallas kernels for 0%

commit v1 on v0

v1 whole, which is shorter than its diff:
```python
import math

import jax
import jax.numpy as jnp
import ml_dtypes
import numpy as np
from jax import lax
from jax.experimental import pallas as pl
from jax.experimental.pallas import tpu as pltpu
from jax.sharding import PartitionSpec as P

JSWEEPS = 3
filter_taps = (0.0625, 0.25, 0.375, 0.25, 0.0625)
band_levels = (12.0, 4.0, 2.5)
rank_level = 2.0
tiny_value = 1e-30

bf16 = jnp.bfloat16
f32 = jnp.float32
ORDER = 32
HALF = 16
OWN = 16
ROWS, COLS = 64, 256
SLOT = 12
PER = 10
EIN, EOUT = 96, 80
WIDE = 384
GRAM_SCALE = float(2.0**32)


def band_matrix(size, dilation):
    out = np.zeros((size, size), np.float64)
    for tap_index, tap in enumerate(filter_taps):
        offset = (tap_index - 2) * dilation
        out += tap * np.eye(size, size, offset)
    return out


def picked(matrix, out_ids, in_ids):
    size = matrix.shape[0]
    out_ok = (out_ids >= 0) & (out_ids < size)
    in_ok = (in_ids >= 0) & (in_ids < size)
    part = matrix[np.clip(out_ids, 0, size - 1)][:, np.clip(in_ids, 0, size - 1)]
    return part * out_ok[:, None] * in_ok[None, :]


def stencil_tables():
    none = -(10**6)
    rows_f, cols_f1, cols_f2, rows_b1, rows_b2, cols_b1, cols_b2 = ([] for _ in range(7))
    for place in range(3):
        a1, a2 = band_matrix(3 * ROWS, 1), band_matrix(3 * ROWS, 2)
        base = place * ROWS
        ein = np.concatenate([base + np.arange(64), base + 64 + np.arange(16), base - 16 + np.arange(16)])
        eout = np.concatenate([base + np.arange(64), base + 64 + np.arange(8), base - 8 + np.arange(8)])
        own = base + np.arange(64)
        fwd = np.concatenate([picked(a1, eout, ein), picked(a2 @ a1, eout, ein)], 0)
        rows_f.append(np.concatenate([fwd, fwd], 1))
        one, two = picked(a1, own, eout), picked(a1 @ a2, own, eout)
        rows_b1.append(np.concatenate([one, one], 1))
        rows_b2.append(np.concatenate([two, two], 1))
        a1, a2 = band_matrix(3 * COLS, 1), band_matrix(3 * COLS, 2)
        base = place * COLS
        right, left = base + COLS + np.arange(SLOT), base - SLOT + np.arange(SLOT)
        pad = np.full(WIDE - COLS - 2 * SLOT, none)
        cin = np.concatenate([base + np.arange(COLS), right, left, pad])
        reach = SLOT // 2
        keep_r = np.where(np.arange(SLOT) < reach, right, none)
        keep_l = np.where(np.arange(SLOT) >= reach, left, none)
        cout = np.concatenate([base + np.arange(COLS), keep_r, keep_l, pad])
        own = base + np.arange(COLS)
        for store, mat in ((cols_f1, a1), (cols_f2, a2 @ a1)):
            part = picked(mat, cout, cin).T
            store.append(np.concatenate([part, part], 0))
        for store, mat in ((cols_b1, a1), (cols_b2, a1 @ a2)):
            part = picked(mat, own, cout).T
            store.append(np.concatenate([part, part], 0))
    return [np.stack(t).astype(ml_dtypes.bfloat16) for t in (rows_f, cols_f1, cols_f2, rows_b1, rows_b2, cols_b1, cols_b2)]


def jacobi_tables():
    players = list(range(ORDER))
    rounds = ORDER - 1
    ints = np.zeros((rounds, 40, 128), np.int32)
    floats = np.zeros((rounds, 16, 128), np.float32)
    for k in range(rounds):
        top = np.array(players[:HALF])
        bottom = np.array([players[ORDER - 1 - i] for i in range(HALF)])
        ints[k, 0:16] = top[:, None]
        ints[k, 16:32] = bottom[:, None]
        partner = np.arange(128)
        partner[top], partner[bottom] = bottom, top
        ints[k, 32:40] = partner[None]
        side = np.zeros(128, np.float32)
        side[top], side[bottom] = 1.0, -1.0
        least = np.zeros(128, np.float32)
        swapped = np.where(top < bottom, 0.0, 1.2e-38)
        least[top], least[bottom] = swapped, swapped
        floats[k, 0:8] = side[None]
        floats[k, 8:16] = least[None]
        players = [players[0], players[-1]] + players[1:-1]
    return ints, floats


def split(x):
    high = x.astype(bf16)
    return high, (x - high.astype(f32)).astype(bf16)


def mm(a, b):
    return jnp.dot(a, b, preferred_element_type=f32)


def pack_kernel(where_ref, x_ref, w_ref, left_ref, right_ref, mine_ref, other_ref):
    chan = where_ref[2]
    lane = lax.broadcasted_iota(jnp.int32, (ROWS, 128), 1)
    for group in range(2):
        low = jnp.zeros((ROWS, 128), f32)
        high = jnp.zeros((ROWS, 128), f32)
        for k in range(PER):
            slot = group * PER + k
            if slot >= OWN + 3:
                break
            tile0 = x_ref[slot, :, 0:128] if slot < OWN else w_ref[slot - OWN, :, 0:128]
            tile1 = x_ref[slot, :, 128:256] if slot < OWN else w_ref[slot - OWN, :, 128:256]
            here = (lane >= SLOT * k) & (lane < SLOT * (k + 1))
            low = jnp.where(here, pltpu.roll(tile0, SLOT * k, 1) if k else tile0, low)
            high = jnp.where(here, pltpu.roll(tile1, (SLOT * k + SLOT) % 128, 1), high)
        left_ref[group] = low
        right_ref[group] = high
    for out_ref, start in ((mine_ref, chan * 32), (other_ref, (1 - chan) * 32)):
        for r in range(4):
            rows = pl.ds(pl.multiple_of(start + 8 * r, 8), 8)
            for c in range(2):
                block = x_ref[8 * c : 8 * c + 8, rows, :]
                out_ref[8 * r : 8 * r + 8, 8 * c : 8 * c + 8, :] = jnp.swapaxes(block, 0, 1)


def gram_kernel(where_ref, own_ref, peer_ref, out_ref):
    first_chan = where_ref[2] == 0
    total = jnp.zeros((64, 64), f32)
    for r in range(0, 32, 4):
        parts = []
        for j in range(4):
            own, peer = own_ref[r + j], peer_ref[r + j]
            both = jnp.concatenate([jnp.where(first_chan, own, peer), jnp.where(first_chan, peer, own)], 0)
            high, low = split(both)
            parts.append(jnp.concatenate([high, low], 0))
        tall = jnp.concatenate(parts, 1)
        total += lax.dot_general(tall, tall, (((1,), (1,)), ((), ())), preferred_element_type=f32)
    gram = (total[0:32, 0:32] + total[32:64, 32:64]) + (total[0:32, 32:64] + total[32:64, 0:32])
    out_ref[...] = jnp.concatenate([gram, jnp.zeros((32, 96), f32)], 1)


def halo_tile(tile_r, tile_l, k):
    lane = lax.broadcasted_iota(jnp.int32, tile_r.shape, 1)
    moved_r = pltpu.roll(tile_r, 128 - SLOT * k, 1) if k else tile_r
    moved_l = pltpu.roll(tile_l, (SLOT + 128 - SLOT * k) % 128, 1) if k != 1 else tile_l
    return jnp.where(lane < SLOT, moved_r, moved_l)


def forward_kernel(where_ref, x_ref, below_ref, above_ref, pr_ref, pl_ref, rows_ref, c1_ref, c2_ref, b_ref, t_ref, ):
    rmat = rows_ref[0]
    for c in range(OWN):
        group, k = c // PER, c % PER
        side = halo_tile(pr_ref[group], pl_ref[group], k)
        side_b = halo_tile(below_ref[OWN + group, :, 0:128], below_ref[OWN + group, :, 128:256], k)
        side_a = halo_tile(above_ref[OWN + group, :, 0:128], above_ref[OWN + group, :, 128:256], k)
        wide = jnp.concatenate(
            [
                jnp.concatenate([x_ref[c], side], 1),
                jnp.concatenate([below_ref[c], side_b], 1),
                jnp.concatenate([above_ref[c], side_a], 1),
            ],
            0,
        )
        high, low = split(wide)
        y = mm(rmat, jnp.concatenate([high, low], 0))
        high, low = split(y)
        z1 = mm(jnp.concatenate([high[:EOUT], low[:EOUT]], 1), c1_ref[0])
        z2 = mm(jnp.concatenate([high[EOUT:], low[EOUT:]], 1), c2_ref[0])
        inner = jnp.concatenate([wide[0:72], wide[88:96]], 0)
        b0, b1 = inner - z1, z1 - z2
        b_ref[c, 0] = b0
        b_ref[c, 1] = b1
        b_ref[c, 2] = z2
        for i, band in enumerate((b0, b1, z2)):
            if c == 0:
                t_ref[i] = band * band
            else:
                t_ref[i] += band * band


def backward_kernel(where_ref, b_ref, t_ref, u_ref, w_ref, below_ref, above_ref, pr_ref, pl_ref,
                    r1_ref, r2_ref, c1_ref, c2_ref, out_ref, f_ref):
    for i in range(3):
        slot = OWN + i
        group, k = slot // PER, slot % PER
        side = halo_tile(pr_ref[group], pl_ref[group], k)
        side_b = halo_tile(below_ref[OWN + group, 0:8, 0:128], below_ref[OWN + group, 0:8, 128:256], k)
        side_a = halo_tile(above_ref[OWN + group, 8:16, 0:128], above_ref[OWN + group, 8:16, 128:256], k)
        weight = jnp.concatenate(
            [
                jnp.concatenate([w_ref[i], side], 1),
                jnp.concatenate([below_ref[18 + i, 0:8], side_b], 1),
                jnp.concatenate([above_ref[18 + i, 8:16], side_a], 1),
            ],
            0,
        )
        level = band_levels[i] * weight
        total = t_ref[i] + u_ref[i]
        f_ref[i] = level * lax.rsqrt(jnp.maximum(jnp.maximum(total, level * level), 1e-30))
    for c in range(OWN):
        d0 = b_ref[c, 0] * f_ref[0]
        d1 = b_ref[c, 1] * f_ref[1]
        d2 = b_ref[c, 2] * f_ref[2]
        high, low = split(d1 - d0)
        y1 = mm(r1_ref[0], jnp.concatenate([high, low], 0))
        high, low = split(d2 - d1)
        y2 = mm(r2_ref[0], jnp.concatenate([high, low], 0))
        high, low = split(y1)
        z = mm(jnp.concatenate([high, low], 1), c1_ref[0])
        high, low = split(y2)
        z += mm(jnp.concatenate([high, low], 1), c2_ref[0])
        out_ref[c] = d0[0:ROWS, 0:COLS] + z


def take(x, ids):
    return jnp.take_along_axis(x, ids, axis=1)


def rotation(gap, cross2, least):
    square = gap * gap + (cross2 * cross2 + 1e-37)
    root = square * lax.rsqrt(square) + tiny_value * GRAM_SCALE
    base = jnp.abs(gap) + root
    inverse = lax.rsqrt(base * base + cross2 * cross2)
    signed = jnp.where(gap >= least, cross2, -cross2)
    return base * inverse, signed * inverse


def sublane_sum(v):
    v = v + pltpu.roll(v, 4, 0)
    v = v + pltpu.roll(v, 2, 0)
    return v + pltpu.roll(v, 1, 0)


def one_round(k, state, ints, floats):
    lane = lax.broadcasted_iota(jnp.int32, (8, 128), 1)
    sub = lax.broadcasted_iota(jnp.int32, (8, 128), 0)
    tops, bottoms = state[:2], state[2:]
    top_ids = (ints[k, 0:8], ints[k, 8:16])
    bottom_ids = (ints[k, 16:24], ints[k, 24:32])
    partner = ints[k, 32:40]
    side, least = floats[k, 0:8], floats[k, 8:16]
    moved_t = [take(v, partner) for v in tops]
    moved_b = [take(v, partner) for v in bottoms]
    by_row = []
    gap = cross = None
    for h in range(2):
        t, b, gt, gb, ti, bi = tops[h], bottoms[h], moved_t[h], moved_b[h], top_ids[h], bottom_ids[h]
        x = take(t, bi)
        by_row.append(rotation(take(b, bi) - take(t, ti), x + x, jnp.where(ti < bi, 0.0, 1.2e-38)))
        on_t, on_b = ti == lane, bi == lane
        part_g = jnp.where(on_t, gb - t, jnp.where(on_b, b - gt, 0.0))
        part_x = jnp.where(on_b, t, jnp.where(on_t, gt, 0.0))
        gap = part_g if gap is None else gap + part_g
        cross = part_x if cross is None else cross + part_x
    gap, cross = sublane_sum(gap), sublane_sum(cross)
    cosine, sine = rotation(gap, cross + cross, least)
    in_gram = lane < ORDER
    cosine = jnp.where(in_gram, cosine, 1.0)
    sine = jnp.where(in_gram, -side * sine, 0.0)
    new_t, new_b = [], []
    for h in range(2):
        c, s = by_row[h]
        t = cosine * tops[h] + sine * moved_t[h]
        b = cosine * bottoms[h] + sine * moved_b[h]
        new_t.append(c * t - s * b)
        new_b.append(s * t + c * b)
    (ta, tb), (ba, bb) = new_t, new_b
    down_a, down_b, first_b = pltpu.roll(ta, 1, 0), pltpu.roll(tb, 1, 0), pltpu.roll(ba, 1, 0)
    up_a, up_b = pltpu.roll(ba, 7, 0), pltpu.roll(bb, 7, 0)
    return (
        jnp.where(sub == 0, ta, jnp.where(sub == 1, first_b, down_a)),
        jnp.where(sub == 0, down_a, down_b),
        jnp.where(sub == 7, up_b, up_a),
        jnp.where(sub == 7, tb, up_b),
    )


def jacobi_kernel(threshold, g_ref, h_ref, ints, floats, out_ref):
    lane = lax.broadcasted_iota(jnp.int32, (8, 128), 1)
    gram = (g_ref[...] + h_ref[...]) * GRAM_SCALE
    labels = [ints[0, 8 * i : 8 * i + 8] for i in range(4)]
    rows = [gram[i : i + 1] for i in range(16)] + [gram[31 - i : 32 - i] for i in range(16)]
    state = tuple(
        jnp.where(lane - ORDER == labels[i], 1.0, jnp.concatenate(rows[8 * i : 8 * i + 8], 0)) for i in range(4)
    )

    def sweep(_, state):
        return lax.fori_loop(0, ORDER - 1, lambda k, s: one_round(k, s, ints, floats), state)

    state = lax.fori_loop(0, JSWEEPS, sweep, state)
    factors = []
    for i in range(4):
        values = take(state[i], labels[i]) * (1.0 / GRAM_SCALE)
        factors.append(1.0 - threshold / jnp.sqrt(jnp.maximum(values, threshold * threshold)))
    whole = jnp.concatenate(state, 0)
    scaled = jnp.concatenate(factors, 0) * whole
    mixing = lax.dot_general(
        scaled, whole, (((0,), (0,)), ((), ())), precision=lax.Precision.HIGHEST, preferred_element_type=f32
    )
    out_ref[...] = pltpu.roll(mixing[ORDER : 2 * ORDER], 128 - ORDER, 1)


def apply_kernel(where_ref, m_ref, mine_ref, other_ref, near_ref, far_ref, out_ref):
    chan = where_ref[2]
    own = m_ref[pl.ds(pl.multiple_of(chan * OWN, OWN), OWN), :]
    first = own[:, 0:16]
    second = own[:, 16:32]
    zero_chan = chan == 0
    mix = jnp.concatenate([jnp.where(zero_chan, first, second), jnp.where(zero_chan, second, first)], 1)
    high, low = split(mix)
    left = jnp.concatenate([high, high, low], 1)
    blank = jnp.zeros_like(left)
    left = jnp.concatenate([jnp.concatenate([left, blank], 1), jnp.concatenate([blank, left], 1)], 0)
    for own_ref, peer_ref, start in ((mine_ref, near_ref, chan * 32), (other_ref, far_ref, (1 - chan) * 32)):
        for r in range(0, 32, 8):
            pieces = []
            for j in range(0, 8, 2):
                stack = []
                for q in range(2):
                    both = jnp.concatenate([own_ref[r + j + q], peer_ref[r + j + q]], 0)
                    high, low = split(both)
                    stack += [high, low, high]
                pieces.append(mm(left, jnp.concatenate(stack, 0)).reshape(2, OWN, COLS))
            block = jnp.concatenate(pieces, 0)
            rows = pl.ds(pl.multiple_of(start + r, 8), 8)
            for c in range(2):
                out_ref[8 * c : 8 * c + 8, rows, :] = jnp.swapaxes(block[:, 8 * c : 8 * c + 8, :], 0, 1)


ROWS_F, COLS_F1, COLS_F2, ROWS_B1, ROWS_B2, COLS_B1, COLS_B2 = stencil_tables()
INTS, FLOATS = jacobi_tables()


def whole(shape):
    return pl.BlockSpec(shape, lambda i, where, n=len(shape): (0,) * n)


def by_row(table):
    return pl.BlockSpec((1, *table.shape[1:]), lambda i, where: (where[0], 0, 0))


def by_col(table):
    return pl.BlockSpec((1, *table.shape[1:]), lambda i, where: (where[1], 0, 0))


def call(kernel, name, where, args, specs, outs, scratch=(), cost=None):
    return pl.pallas_call(
        kernel,
        out_shape=[jax.ShapeDtypeStruct(s, f32) for s in outs],
        grid_spec=pltpu.PrefetchScalarGridSpec(
            num_scalar_prefetch=1,
            grid=(1,),
            in_specs=[whole(a.shape) if s is None else s for a, s in zip(args, specs)],
            out_specs=[whole(s) for s in outs],
            scratch_shapes=list(scratch),
        ),
        compiler_params=pltpu.CompilerParams(vmem_limit_bytes=50 * 2**20),
        cost_estimate=cost,
        name=name,
    )(where, *args)


def shards(x, w):
    frow, fcol, chan = (lax.axis_index(a) for a in ("frow", "fcol", "chan"))
    last_r, last_c = lax.axis_size("frow") - 1, lax.axis_size("fcol") - 1

    def place(i, last):
        return jnp.where(i == 0, 0, jnp.where(i == last, 2, 1))

    where = jnp.stack([place(frow, last_r), place(fcol, last_c), chan]).astype(jnp.int32)
    up = [(i, i + 1) for i in range(7)]
    down = [(i + 1, i) for i in range(7)]
    swap = [(0, 1), (1, 0)]
    tile = (2, ROWS, 128)
    half = (32, OWN, COLS)
    left, right, mine, other = call(
        pack_kernel, "pack", where, (x, w), (None, None), (tile, tile, half, half)
    )
    near = lax.ppermute(other, "chan", swap)
    from_right = lax.ppermute(left, "fcol", down)
    from_left = lax.ppermute(right, "fcol", up)
    far = lax.ppermute(mine, "chan", swap)
    sides = jnp.concatenate([from_right, from_left], 2)

    def edge(rows):
        return jnp.concatenate([x[:, rows], sides[:, rows], w[:, rows]], 0)

    below = lax.ppermute(edge(slice(0, 16)), "frow", down)
    above = lax.ppermute(edge(slice(48, 64)), "frow", up)
    (gram,) = call(gram_kernel, "gram", where, (mine, near), (None, None), ((ORDER, 128),))
    gram_peer = lax.ppermute(gram, "chan", swap)
    bands, totals = call(
        forward_kernel,
        "forward",
        where,
        (x, below, above, from_right, from_left, ROWS_F, COLS_F1, COLS_F2),
        (None,) * 5 + (by_row(ROWS_F), by_col(COLS_F1), by_col(COLS_F2)),
        ((OWN, 3, EOUT, WIDE), (3, EOUT, WIDE)),
    )
    totals_peer = lax.ppermute(totals, "chan", swap)
    threshold = rank_level * math.sqrt(ROWS * COLS)
    mixing = pl.pallas_call(
        lambda *refs: jacobi_kernel(threshold, *refs),
        out_shape=jax.ShapeDtypeStruct((ORDER, 128), f32),
        name="jacobi",
    )(gram, gram_peer, INTS, FLOATS)
    (back,) = call(
        backward_kernel,
        "backward",
        where,
        (bands, totals, totals_peer, w, below, above, from_right, from_left, ROWS_B1, ROWS_B2, COLS_B1, COLS_B2),
        (None,) * 8 + (by_row(ROWS_B1), by_row(ROWS_B2), by_col(COLS_B1), by_col(COLS_B2)),
        ((OWN, ROWS, COLS),),
        (pltpu.VMEM((3, EOUT, WIDE), f32),),
    )
    (low,) = call(
        apply_kernel, "apply", where, (mixing, mine, other, near, far), (None,) * 5, ((OWN, ROWS, COLS),)
    )
    return back, low


def solution(mesh):
    return jax.shard_map(
        shards,
        mesh=mesh,
        in_specs=(P("chan", "frow", "fcol"), P(None, "frow", "fcol")),
        out_specs=(P("chan", "frow", "fcol"), P("chan", "frow", "fcol")),
        check_vma=False,
    )
```

time: 840 us -> 83.1 us (0.10)
  the two profiles are of different devices: /device:TPU:7 before, /device:TPU:25 now
where the time goes in v1:
time: 83.1 us; the launch traced here: 82.8 us
  Pallas kernels  35.1 us (42%)
  waiting for transfers between devices  25.5 us (31%)
  starting transfers between devices  17.6 us (21%)
  local copies, waits for them, and re-layouts  3.68 us (4%)
    pallas_call x5, Pallas kernels, call(): pl.pallas_call(kernel, out_shape=[jax.ShapeDtypeStruct(s, f32) for s in o...  21.9 us
    ppermute x1, waiting for transfers between devices, shards(): gram_peer = lax.ppermute(gram, 'chan', swap)  16.2 us
    pallas_call x1, Pallas kernels, shards(): pl.pallas_call(lambda *refs: jacobi_kernel(threshold, *refs), out_shape=j...  13.2 us
    ppermute x1, waiting for transfers between devices, shards(): from_left = lax.ppermute(right, 'fcol', up)  6.61 us
    ppermute x1, starting transfers between devices, shards(): from_right = lax.ppermute(left, 'fcol', down)  5.19 us
    ppermute x1, starting transfers between devices, shards(): below = lax.ppermute(edge(slice(0, 16)), 'frow', down)  4.01 us
    unnamed x21, local copies, waits for them, and re-layouts  3.62 us
    ppermute x1, starting transfers between devices, shards(): above = lax.ppermute(edge(slice(48, 64)), 'frow', up)  3.44 us
  transfers between devices with their start and end apart: 8, of which 5 were waited for; matrix products, arithmetic and copies ran while one was open for 0% of the time, Pallas kernels for 32%

profile of v1, /device:TPU:25, one launch (start us, length us, event | category | flops | bytes accessed | tf_op | source)
XLA Modules:
  0.0 82.8 jit_solution(17400746669214438551)
XLA Ops:
  0.6 0.1 pad_add_fusion.where_ref
  0.7 1.2 %copy-done = f32[16,64,256]{2,1,0:T(8,128)S(1)} copy-done((f32[16,64,256]{2,1,0:T(8,128)S(1)}, f32[16,64,256]{2,1,0:T(8,128)}, u32[]{:S(2)}) %copy-start) | copy-done | bytes 1048600
  2.0 0.9 %copy-done.1 = f32[3,64,256]{2,1,0:T(8,128)S(1)} copy-done((f32[3,64,256]{2,1,0:T(8,128)S(1)}, f32[3,64,256]{2,1,0:T(8,128)}, u32[]{:S(2)}) %copy-start.1) | copy-done | bytes 196632
  2.9 1.0 %pack.1 = (f32[2,64,128]{2,1,0:T(8,128)S(1)}, f32[2,64,128]{2,1,0:T(8,128)S(1)}, f32[32,16,256]{2,1,0:T(8,128)S(1)}, f32[32,16,256]{2,1,0:T(8,128)S(1)}) custom-call(s32[3]{0:T(128)S(1)} %pad_add_fusion.where_ref, f32[16,64,256]{2,1,0:T(8,128)S(1)} %copy-done, f32[3,64,256]{2,1,0:T(8,128)S(1)} %copy-done.1), custom_call_target="tpu_custom_call" | custom-call | tf_op jit(solution)/shard_map/pack/pallas_call | solution.py:359
  3.9 0.0 copy-start.4
  3.9 5.2 %collective-permute-start = (f32[2,64,128]{2,1,0:T(8,128)S(1)}, f32[2,64,128]{2,1,0:T(8,128)S(1)}, u32[]{:S(2)}, u32[]{:S(2)}) collective-permute-start(f32[2,64,128]{2,1,0:T(8,128)S(1)} %get-tuple-element.8), channel_id=1, source_target_pairs={{2,0},{4,2},{6,4},{8,6},{10,8},{12,10},{14,12},{3,1},{5,3},{7,5},{... | collective-permute-start | bytes 196616 | tf_op jit(solution)/shard_map/ppermute | solution.py:392
  9.1 1.9 %collective-permute-start.1 = (f32[2,64,128]{2,1,0:T(8,128)S(1)}, f32[2,64,128]{2,1,0:T(8,128)S(1)}, u32[]{:S(2)}, u32[]{:S(2)}) collective-permute-start(f32[2,64,128]{2,1,0:T(8,128)S(1)} %get-tuple-element.9), channel_id=1, source_target_pairs={{0,2},{2,4},{4,6},{6,8},{8,10},{10,12},{12,14},{1,3},{3,5},{5,7},{... | collective-permute-start | bytes 196616 | tf_op jit(solution)/shard_map/ppermute | solution.py:393
  11.1 6.6 %collective-permute-done.1.pl_ref = f32[2,64,128]{2,1,0:T(8,128)S(1)} collective-permute-done((f32[2,64,128]{2,1,0:T(8,128)S(1)}, f32[2,64,128]{2,1,0:T(8,128)S(1)}, u32[]{:S(2)}, u32[]{:S(2)}) %collective-permute-start.1) | collective-permute-done | bytes 65568 | tf_op jit(solution)/shard_map/ppermute | solution.py:393
  17.8 4.0 %collective-permute-start.2 = (f32[21,16,256]{2,1,0:T(8,128)S(1)}, f32[21,16,256]{2,1,0:T(8,128)S(1)}, u32[]{:S(2)}, u32[]{:S(2)}) collective-permute-start(f32[21,16,256]{2,1,0:T(8,128)S(1)} %pad_maximum_fusion), channel_id=1, source_target_pairs={{16,0},{32,16},{48,32},{64,48},{80,64},{96,80},{112,96},{17,1},{33... | collective-permute-start | bytes 1032200 | tf_op jit(solution)/shard_map/ppermute | solution.py:400
  21.9 3.4 %collective-permute-start.3 = (f32[21,16,256]{2,1,0:T(8,128)S(1)}, f32[21,16,256]{2,1,0:T(8,128)S(1)}, u32[]{:S(2)}, u32[]{:S(2)}) collective-permute-start(f32[21,16,256]{2,1,0:T(8,128)S(1)} %pad_maximum_fusion.1), channel_id=1, source_target_pairs={{0,16},{16,32},{32,48},{48,64},{64,80},{80,96},{96,112},{1,17},{17... | collective-permute-start | bytes 1032200 | tf_op jit(solution)/shard_map/ppermute | solution.py:401
  25.3 0.1 collective-permute-start.5
  25.4 1.5 %collective-permute-start.7 = (f32[32,16,256]{2,1,0:T(8,128)S(1)}, f32[32,16,256]{2,1,0:T(8,128)S(1)}, u32[]{:S(2)}, u32[]{:S(2)}) collective-permute-start(f32[32,16,256]{2,1,0:T(8,128)S(1)} %get-tuple-element.12.own_ref.mine_ref), channel_id=1, source_target_pairs={{0,1},{1,0},{2,3},{3,2},{4,5},{5,4},{6,7},{7,6},{8,9},{9,8},{10,11... | collective-permute-start | bytes 1572872 | tf_op jit(solution)/shard_map/ppermute | solution.py:394
  26.9 1.7 %collective-permute-done.2.below_ref = f32[21,16,256]{2,1,0:T(8,128)S(1)} collective-permute-done((f32[21,16,256]{2,1,0:T(8,128)S(1)}, f32[21,16,256]{2,1,0:T(8,128)S(1)}, u32[]{:S(2)}, u32[]{:S(2)}) %collective-permute-start.2) | collective-permute-done | bytes 344096 | tf_op jit(solution)/shard_map/ppermute | solution.py:400
  28.6 0.9 %collective-permute-done.3.above_ref = f32[21,16,256]{2,1,0:T(8,128)S(1)} collective-permute-done((f32[21,16,256]{2,1,0:T(8,128)S(1)}, f32[21,16,256]{2,1,0:T(8,128)S(1)}, u32[]{:S(2)}, u32[]{:S(2)}) %collective-permute-start.3) | collective-permute-done | bytes 344096 | tf_op jit(solution)/shard_map/ppermute | solution.py:401
  29.5 9.7 %forward.1 = (f32[16,3,80,384]{3,2,1,0:T(8,128)}, f32[3,80,384]{2,1,0:T(8,128)S(1)}) custom-call(s32[3]{0:T(128)S(1)} %pad_add_fusion.where_ref, f32[16,64,256]{2,1,0:T(8,128)S(1)} %copy-done, f32[21,16,256]{2,1,0:T(8,128)S(1)} %collective-permute-done.2.below_ref, f32[21,16,256]{2,1,0:T(8,128)S(1)} %collective-permute-done.3.above_ref, ...), custom_call_target="tpu_custom_call" | custom-call | tf_op jit(solution)/shard_map/forward/pallas_call | solution.py:359
  39.2 0.1 collective-permute-done.5.peer_ref.near_ref
  39.3 1.1 %gram.1.refs_0_ = f32[32,128]{1,0:T(8,128)S(1)} custom-call(s32[3]{0:T(128)S(1)} %pad_add_fusion.where_ref, f32[32,16,256]{2,1,0:T(8,128)S(1)} %get-tuple-element.12.own_ref.mine_ref, f32[32,16,256]{2,1,0:T(8,128)S(1)} %collective-permute-done.5.peer_ref.near_ref), custom_call_target="tpu_custom_call" | custom-call | tf_op jit(solution)/shard_map/gram/pallas_call | solution.py:359
  40.4 1.5 %collective-permute-start.6 = (f32[32,128]{1,0:T(8,128)S(1)}, f32[32,128]{1,0:T(8,128)S(1)}, u32[]{:S(2)}, u32[]{:S(2)}) collective-permute-start(f32[32,128]{1,0:T(8,128)S(1)} %gram.1.refs_0_), channel_id=1, source_target_pairs={{0,1},{1,0},{2,3},{3,2},{4,5},{5,4},{6,7},{7,6},{8,9},{9,8},{10,11... | collective-permute-start | bytes 49160 | tf_op jit(solution)/shard_map/ppermute | solution.py:403
  41.8 16.2 %collective-permute-done.6.refs_1_ = f32[32,128]{1,0:T(8,128)S(1)} collective-permute-done((f32[32,128]{1,0:T(8,128)S(1)}, f32[32,128]{1,0:T(8,128)S(1)}, u32[]{:S(2)}, u32[]{:S(2)}) %collective-permute-start.6) | collective-permute-done | bytes 16416 | tf_op jit(solution)/shard_map/ppermute | solution.py:403
  58.0 0.6 copy-done.9
  58.6 13.2 %jacobi.1.m_ref = f32[32,128]{1,0:T(8,128)} custom-call(f32[32,128]{1,0:T(8,128)} %copy-done.8, f32[32,128]{1,0:T(8,128)} %copy-done.9, s32[31,40,128]{2,1,0:T(8,128)} %constant.41.clone.refs_2_, f32[31,16,128]{2,1,0:T(8,128)} %constant.42.clone.refs_3_), custom_call_target="tpu_custom_call" | custom-call | tf_op jit(solution)/shard_map/jacobi/pallas_call | solution.py:414
  71.8 0.8 copy-done.7
  72.7 2.4 %apply.1 = f32[16,64,256]{2,1,0:T(8,128)} custom-call(s32[3]{0:T(128)S(1)} %pad_add_fusion.where_ref, f32[32,128]{1,0:T(8,128)S(1)} %copy-done.7, f32[32,16,256]{2,1,0:T(8,128)S(1)} %get-tuple-element.12.own_ref.mine_ref, f32[32,16,256]{2,1,0:T(8,128)S(1)} %get-tuple-element.13.other_ref, f32[32,16,256]{2,1,0:T(8,128)S(1)} %collective-permute-done.5.peer_ref.near_ref, ...), custom_call_target="tpu_custom_call" | custom-call | tf_op jit(solution)/shard_map/apply/pallas_call | solution.py:359
  75.1 7.7 %backward.1 = f32[16,64,256]{2,1,0:T(8,128)} custom-call(s32[3]{0:T(128)S(1)} %pad_add_fusion.where_ref, f32[16,3,80,384]{3,2,1,0:T(8,128)} %get-tuple-element.10.b_ref, f32[3,80,384]{2,1,0:T(8,128)S(1)} %get-tuple-element.11.t_ref, f32[3,80,384]{2,1,0:T(8,128)} %collective-permute-done.4.u_ref, f32[3,64,256]{2,1,0:T(8,128)S(1)} %copy-done.2, ...), custom_call_target="tpu_custom_call" | custom-call | tf_op jit(solution)/shard_map/backward/pallas_call | solution.py:359
  (26 shorter events, 0.2 us)
Async XLA Ops:
  0.7 1.2 %copy-start = (f32[16,64,256]{2,1,0:T(8,128)S(1)}, f32[16,64,256]{2,1,0:T(8,128)}, u32[]{:S(2)}) copy-start(f32[16,64,256]{2,1,0:T(8,128)} %x_ref.3) | copy-start | bytes 3145732
  2.0 0.9 %copy-start.1 = (f32[3,64,256]{2,1,0:T(8,128)S(1)}, f32[3,64,256]{2,1,0:T(8,128)}, u32[]{:S(2)}) copy-start(f32[3,64,256]{2,1,0:T(8,128)} %w_ref.3) | copy-start | bytes 589828
  3.9 25.6 %copy-start.4 = (bf16[3,160,192]{2,1,0:T(8,128)(2,1)S(1)}, bf16[3,160,192]{2,1,0:T(8,128)(2,1)}, u32[]{:S(2)}) copy-start(bf16[3,160,192]{2,1,0:T(8,128)(2,1)} %constant.38.clone.rows_ref) | copy-start | bytes 552964
  3.9 7.2 %collective-permute-start = (f32[2,64,128]{2,1,0:T(8,128)S(1)}, f32[2,64,128]{2,1,0:T(8,128)S(1)}, u32[]{:S(2)}, u32[]{:S(2)}) collective-permute-start(f32[2,64,128]{2,1,0:T(8,128)S(1)} %get-tuple-element.8), channel_id=1, source_target_pairs={{2,0},{4,2},{6,4},{8,6},{10,8},{12,10},{14,12},{3,1},{5,3},{7,5},{... | collective-permute-start | bytes 196616 | tf_op jit(solution)/shard_map/ppermute | solution.py:392
  9.1 8.6 %collective-permute-start.1 = (f32[2,64,128]{2,1,0:T(8,128)S(1)}, f32[2,64,128]{2,1,0:T(8,128)S(1)}, u32[]{:S(2)}, u32[]{:S(2)}) collective-permute-start(f32[2,64,128]{2,1,0:T(8,128)S(1)} %get-tuple-element.9), channel_id=1, source_target_pairs={{0,2},{2,4},{4,6},{6,8},{8,10},{10,12},{12,14},{1,3},{3,5},{5,7},{... | collective-permute-start | bytes 196616 | tf_op jit(solution)/shard_map/ppermute | solution.py:393
  17.8 10.8 %collective-permute-start.2 = (f32[21,16,256]{2,1,0:T(8,128)S(1)}, f32[21,16,256]{2,1,0:T(8,128)S(1)}, u32[]{:S(2)}, u32[]{:S(2)}) collective-permute-start(f32[21,16,256]{2,1,0:T(8,128)S(1)} %pad_maximum_fusion), channel_id=1, source_target_pairs={{16,0},{32,16},{48,32},{64,48},{80,64},{96,80},{112,96},{17,1},{33... | collective-permute-start | bytes 1032200 | tf_op jit(solution)/shard_map/ppermute | solution.py:400
  21.9 7.6 %collective-permute-start.3 = (f32[21,16,256]{2,1,0:T(8,128)S(1)}, f32[21,16,256]{2,1,0:T(8,128)S(1)}, u32[]{:S(2)}, u32[]{:S(2)}) collective-permute-start(f32[21,16,256]{2,1,0:T(8,128)S(1)} %pad_maximum_fusion.1), channel_id=1, source_target_pairs={{0,16},{16,32},{32,48},{48,64},{64,80},{80,96},{96,112},{1,17},{17... | collective-permute-start | bytes 1032200 | tf_op jit(solution)/shard_map/ppermute | solution.py:401
  25.3 14.0 %collective-permute-start.5 = (f32[32,16,256]{2,1,0:T(8,128)S(1)}, f32[32,16,256]{2,1,0:T(8,128)S(1)}, u32[]{:S(2)}, u32[]{:S(2)}) collective-permute-start(f32[32,16,256]{2,1,0:T(8,128)S(1)} %get-tuple-element.13.other_ref), channel_id=1, source_target_pairs={{0,1},{1,0},{2,3},{3,2},{4,5},{5,4},{6,7},{7,6},{8,9},{9,8},{10,11... | collective-permute-start | bytes 1572872 | tf_op jit(solution)/shard_map/ppermute | solution.py:391
  25.4 46.4 %collective-permute-start.7 = (f32[32,16,256]{2,1,0:T(8,128)S(1)}, f32[32,16,256]{2,1,0:T(8,128)S(1)}, u32[]{:S(2)}, u32[]{:S(2)}) collective-permute-start(f32[32,16,256]{2,1,0:T(8,128)S(1)} %get-tuple-element.12.own_ref.mine_ref), channel_id=1, source_target_pairs={{0,1},{1,0},{2,3},{3,2},{4,5},{5,4},{6,7},{7,6},{8,9},{9,8},{10,11... | collective-permute-start | bytes 1572872 | tf_op jit(solution)/shard_map/ppermute | solution.py:394
  39.2 35.9 %collective-permute-start.4 = (f32[3,80,384]{2,1,0:T(8,128)S(1)}, f32[3,80,384]{2,1,0:T(8,128)}, u32[]{:S(2)}, u32[]{:S(2)}) collective-permute-start(f32[3,80,384]{2,1,0:T(8,128)S(1)} %get-tuple-element.11.t_ref), channel_id=1, source_target_pairs={{0,1},{1,0},{2,3},{3,2},{4,5},{5,4},{6,7},{7,6},{8,9},{9,8},{10,11... | collective-permute-start | bytes 1105928 | tf_op jit(solution)/shard_map/ppermute | solution.py:412
  40.4 17.6 %copy-start.8 = (f32[32,128]{1,0:T(8,128)}, f32[32,128]{1,0:T(8,128)S(1)}, u32[]{:S(2)}) copy-start(f32[32,128]{1,0:T(8,128)S(1)} %gram.1.refs_0_) | copy-start | bytes 49156
  40.4 17.6 %collective-permute-start.6 = (f32[32,128]{1,0:T(8,128)S(1)}, f32[32,128]{1,0:T(8,128)S(1)}, u32[]{:S(2)}, u32[]{:S(2)}) collective-permute-start(f32[32,128]{1,0:T(8,128)S(1)} %gram.1.refs_0_), channel_id=1, source_target_pairs={{0,1},{1,0},{2,3},{3,2},{4,5},{5,4},{6,7},{7,6},{8,9},{9,8},{10,11... | collective-permute-start | bytes 49160 | tf_op jit(solution)/shard_map/ppermute | solution.py:403
  58.0 0.6 copy-start.9
  71.8 3.3 %copy-start.2 = (f32[3,64,256]{2,1,0:T(8,128)S(1)}, f32[3,64,256]{2,1,0:T(8,128)}, u32[]{:S(2)}) copy-start(f32[3,64,256]{2,1,0:T(8,128)} %w_ref.3) | copy-start | bytes 589828
  71.8 3.3 %copy-start.3 = (bf16[3,768,256]{2,1,0:T(8,128)(2,1)S(1)}, bf16[3,768,256]{2,1,0:T(8,128)(2,1)}, u32[]{:S(2)}) copy-start(bf16[3,768,256]{2,1,0:T(8,128)(2,1)} %constant.45.clone.c1_ref) | copy-start | bytes 3538948
  71.8 3.3 %copy-start.5 = (bf16[3,64,160]{2,1,0:T(8,128)(2,1)S(1)}, bf16[3,64,160]{2,1,0:T(8,128)(2,1)}, u32[]{:S(2)}) copy-start(bf16[3,64,160]{2,1,0:T(8,128)(2,1)} %constant.44.clone.r2_ref) | copy-start | bytes 184324
  71.8 3.3 %copy-start.6 = (bf16[3,64,160]{2,1,0:T(8,128)(2,1)S(1)}, bf16[3,64,160]{2,1,0:T(8,128)(2,1)}, u32[]{:S(2)}) copy-start(bf16[3,64,160]{2,1,0:T(8,128)(2,1)} %constant.43.clone.r1_ref) | copy-start | bytes 184324
  71.8 0.8 %copy-start.7 = (f32[32,128]{1,0:T(8,128)S(1)}, f32[32,128]{1,0:T(8,128)}, u32[]{:S(2)}) copy-start(f32[32,128]{1,0:T(8,128)} %jacobi.1.m_ref) | copy-start | bytes 49156

commit v2 on v1

v2 whole, which is shorter than its diff:
```python
import math

import jax
import jax.numpy as jnp
import ml_dtypes
import numpy as np
from jax import lax
from jax.experimental import pallas as pl
from jax.experimental.pallas import tpu as pltpu
from jax.sharding import PartitionSpec as P

JSWEEPS = 3
filter_taps = (0.0625, 0.25, 0.375, 0.25, 0.0625)
band_levels = (12.0, 4.0, 2.5)
rank_level = 2.0
tiny_value = 1e-30

bf16 = jnp.bfloat16
f32 = jnp.float32
ORDER = 32
HALF = 16
OWN = 16
ROWS, COLS = 64, 256
SLOT = 12
PER = 10
EIN, EOUT = 96, 80
WIDE = 384
GRAM_SCALE = float(2.0**32)
VFIRST = 24
CB = 8


def band_matrix(size, dilation):
    out = np.zeros((size, size), np.float64)
    for tap_index, tap in enumerate(filter_taps):
        offset = (tap_index - 2) * dilation
        out += tap * np.eye(size, size, offset)
    return out


def picked(matrix, out_ids, in_ids):
    size = matrix.shape[0]
    out_ok = (out_ids >= 0) & (out_ids < size)
    in_ok = (in_ids >= 0) & (in_ids < size)
    part = matrix[np.clip(out_ids, 0, size - 1)][:, np.clip(in_ids, 0, size - 1)]
    return part * out_ok[:, None] * in_ok[None, :]


def stencil_tables():
    none = -(10**6)
    rows_f, cols_f1, cols_f2, rows_b1, rows_b2, cols_b1, cols_b2 = ([] for _ in range(7))
    for place in range(3):
        a1, a2 = band_matrix(3 * ROWS, 1), band_matrix(3 * ROWS, 2)
        base = place * ROWS
        ein = np.concatenate([base + np.arange(64), base + 64 + np.arange(16), base - 16 + np.arange(16)])
        eout = np.concatenate([base + np.arange(64), base + 64 + np.arange(8), base - 8 + np.arange(8)])
        own = base + np.arange(64)
        fwd = np.concatenate([picked(a1, eout, ein), picked(a2 @ a1, eout, ein)], 0)
        rows_f.append(np.concatenate([fwd, fwd], 1))
        one, two = picked(a1, own, eout), picked(a1 @ a2, own, eout)
        rows_b1.append(np.concatenate([one, one], 1))
        rows_b2.append(np.concatenate([two, two], 1))
        a1, a2 = band_matrix(3 * COLS, 1), band_matrix(3 * COLS, 2)
        base = place * COLS
        right, left = base + COLS + np.arange(SLOT), base - SLOT + np.arange(SLOT)
        pad = np.full(WIDE - COLS - 2 * SLOT, none)
        cin = np.concatenate([base + np.arange(COLS), right, left, pad])
        reach = SLOT // 2
        keep_r = np.where(np.arange(SLOT) < reach, right, none)
        keep_l = np.where(np.arange(SLOT) >= reach, left, none)
        cout = np.concatenate([base + np.arange(COLS), keep_r, keep_l, pad])
        own = base + np.arange(COLS)
        for store, mat in ((cols_f1, a1), (cols_f2, a2 @ a1)):
            store.append(picked(mat, cout, cin).T)
        for store, mat in ((cols_b1, a1), (cols_b2, a1 @ a2)):
            store.append(picked(mat, own, cout).T)

    def merged(parts, width):
        padded = [np.pad(np.stack(p), ((0, 0), (0, 0), (0, width - p[0].shape[1]))) for p in parts]
        return np.concatenate(padded, 1).astype(ml_dtypes.bfloat16)

    return merged((cols_f1, cols_f2, rows_f), WIDE), merged((cols_b1, cols_b2, rows_b1, rows_b2), COLS)


def jacobi_tables():
    players = list(range(ORDER))
    least = np.zeros((ORDER - 1, HALF, 128), np.float32)
    for k in range(ORDER - 1):
        for i in range(HALF):
            least[k, i] = 0.0 if players[i] < players[ORDER - 1 - i] else 1.2e-38
        players = [players[0], players[-1]] + players[1:-1]
    return least


def split(x):
    high = x.astype(bf16)
    return high, (x - high.astype(f32)).astype(bf16)


def mm(a, b):
    return jnp.dot(a, b, preferred_element_type=f32)


def cut_kernel(where_ref, x_ref, w_ref, half_ref, even_ref, odd_ref, sems):
    start = pl.multiple_of((1 - where_ref[2]) * 32, 32)
    own = pl.multiple_of(where_ref[2] * 32, 32)
    copies = [
        (x_ref.at[:, pl.ds(start, 32), :], half_ref.at[:, 0:32, :]),
        (x_ref.at[:, pl.ds(own, 8), :], half_ref.at[:, 32:40, :]),
    ]
    for out_ref, parity in ((even_ref, 1 - where_ref[3]), (odd_ref, where_ref[3])):
        rows = pl.ds(pl.multiple_of(parity * 48, 16), 16)
        copies.append((x_ref.at[:, rows, :], out_ref.at[0:OWN]))
        copies.append((w_ref.at[:, rows, :], out_ref.at[OWN : OWN + 3]))
    copies = [pltpu.make_async_copy(a, b, sems.at[i]) for i, (a, b) in enumerate(copies)]
    for copy in copies:
        copy.start()
    for copy in copies:
        copy.wait()


def pack_rows(tiles, count, even_ref, odd_ref, at, parity):
    lane = lax.broadcasted_iota(jnp.int32, (count, 128), 1)
    for group in range(2):
        low = jnp.zeros((count, 128), f32)
        high = jnp.zeros((count, 128), f32)
        for k in range(PER):
            slot = group * PER + k
            if slot >= OWN + 3:
                break
            tile0, tile1 = tiles(slot)
            here = (lane >= SLOT * k) & (lane < SLOT * (k + 1))
            low = jnp.where(here, pltpu.roll(tile0, SLOT * k, 1) if k else tile0, low)
            high = jnp.where(here, pltpu.roll(tile1, (SLOT * k + SLOT) % 128, 1), high)
        even_ref[group, at : at + count] = jnp.where(parity == 0, high, low)
        odd_ref[group, at : at + count] = jnp.where(parity == 0, low, high)


def pack_kernel(where_ref, x_ref, w_ref, even_ref, odd_ref, mine_ref, other_ref, held, sems):
    chan = where_ref[2]
    copies = [
        pltpu.make_async_copy(x_ref.at[4 * i : 4 * i + 4], held.at[4 * i : 4 * i + 4], sems.at[i]) for i in range(4)
    ]
    copies.append(pltpu.make_async_copy(w_ref, held.at[OWN : OWN + 3], sems.at[4]))
    for copy in copies:
        copy.start()

    def tiles(slot):
        if slot % 4 == 0:
            copies[slot // 4].wait()
        return held[slot, :, 0:128], held[slot, :, 128:256]

    pack_rows(tiles, ROWS, even_ref, odd_ref, 0, where_ref[4])
    for out_ref, start in ((mine_ref, chan * 32), (other_ref, (1 - chan) * 32)):
        for r in range(4):
            rows = pl.ds(pl.multiple_of(start + 8 * r, 8), 8)
            for c in range(2):
                block = held[8 * c : 8 * c + 8, rows, :]
                out_ref[8 * r : 8 * r + 8, 8 * c : 8 * c + 8, :] = jnp.swapaxes(block, 0, 1)


def pack_halo_kernel(where_ref, old_e, old_o, rows_e, rows_o, even_ref, odd_ref):
    even_ref[:, 0:ROWS] = old_e[:, 0:ROWS]
    odd_ref[:, 0:ROWS] = old_o[:, 0:ROWS]
    upper = where_ref[3] == 0
    for at, flip in ((ROWS, False), (ROWS + 16, True)):

        def tiles(slot, flip=flip):
            one, two = (rows_o, rows_e) if flip else (rows_e, rows_o)
            both = jnp.where(upper, one[slot], two[slot])
            return both[:, 0:128], both[:, 128:256]

        pack_rows(tiles, 16, even_ref, odd_ref, at, where_ref[4])


def gram_kernel(where_ref, own_ref, peer_ref, send_ref, near_ref):
    first_chan = where_ref[2] == 0
    for r in range(5):
        for c in range(2):
            block = peer_ref[8 * c : 8 * c + 8, 8 * r : 8 * r + 8, :]
            near_ref[8 * r : 8 * r + 8, 8 * c : 8 * c + 8, :] = jnp.swapaxes(block, 0, 1)
    total = jnp.zeros((64, 64), f32)
    for r in range(0, 32, 4):
        parts = []
        for j in range(4):
            own, peer = own_ref[r + j], near_ref[r + j]
            both = jnp.concatenate([jnp.where(first_chan, own, peer), jnp.where(first_chan, peer, own)], 0)
            high, low = split(both)
            parts.append(jnp.concatenate([high, low], 0))
        tall = jnp.concatenate(parts, 1)
        total += lax.dot_general(tall, tall, (((1,), (1,)), ((), ())), preferred_element_type=f32)
    gram = (total[0:32, 0:32] + total[32:64, 32:64]) + (total[0:32, 32:64] + total[32:64, 0:32])
    send_ref[...] = jnp.concatenate([gram, jnp.zeros((32, 96), f32)], 1)


def sorted_pair(parity, even, odd):
    return jnp.where(parity == 0, even, odd), jnp.where(parity == 0, odd, even)


def doubled(tables, at, out_ref):
    out_ref[0:WIDE] = tables[at : at + WIDE]
    out_ref[WIDE:] = tables[at : at + WIDE]


def halo_tile(tile_r, tile_l, k):
    lane = lax.broadcasted_iota(jnp.int32, tile_r.shape, 1)
    moved_r = pltpu.roll(tile_r, 128 - SLOT * k, 1) if k else tile_r
    moved_l = pltpu.roll(tile_l, (SLOT + 128 - SLOT * k) % 128, 1) if k != 1 else tile_l
    return jnp.where(lane < SLOT, moved_r, moved_l)


def forward_kernel(where_ref, x_ref, re_ref, ro_ref, ce_ref, co_ref, rmat, c1_ref, c2_ref, bands, totals, c0, wide_ref, s_ref):
    for j in range(CB):
        c = c0 + j
        group, k = c // PER, c % PER
        right, left = sorted_pair(where_ref[4], ce_ref[group], co_ref[group])
        below, above = sorted_pair(where_ref[3], re_ref[c], ro_ref[c])
        side = halo_tile(right, left, k)
        wide = jnp.concatenate([jnp.concatenate([x_ref[c], below, above], 0), side], 1)
        wide_ref[j, 0:72] = wide[0:72]
        wide_ref[j, 72:80] = wide[88:96]
        high, low = split(wide)
        y = mm(rmat, jnp.concatenate([high, low], 0))
        high, low = split(y)
        rows = slice(j * EOUT, (j + 1) * EOUT)
        s_ref[0, rows, 0:WIDE] = high[:EOUT]
        s_ref[0, rows, WIDE:] = low[:EOUT]
        s_ref[1, rows, 0:WIDE] = high[EOUT:]
        s_ref[1, rows, WIDE:] = low[EOUT:]
    z1 = mm(s_ref[0], c1_ref[...])
    z2 = mm(s_ref[1], c2_ref[...])
    for j in range(CB):
        rows = slice(j * EOUT, (j + 1) * EOUT)
        one, two = z1[rows], z2[rows]
        b0, b1 = wide_ref[j] - one, one - two
        bands[j, 0] = b0
        bands[j, 1] = b1
        bands[j, 2] = two
        for i, band in enumerate((b0, b1, two)):
            if c0 + j == 0:
                totals[i] = band * band
            else:
                totals[i] += band * band


def forward_steps(where_ref, x_ref, re_ref, ro_ref, ce_ref, co_ref, cols_ref, rows_ref,
                  b_ref, t_ref, wide_ref, s_ref, totals, d1_ref, d2_ref):
    @pl.when(pl.program_id(0) == 0)
    def _():
        doubled(cols_ref.at[0], 0, d1_ref)
        doubled(cols_ref.at[0], WIDE, d2_ref)

    for step in range(OWN // CB):

        @pl.when(pl.program_id(0) == step)
        def _():
            forward_kernel(where_ref, x_ref, re_ref, ro_ref, ce_ref, co_ref, rows_ref[0, 2 * WIDE :, 0 : 2 * EIN], d1_ref, d2_ref,
                           b_ref, totals, step * CB, wide_ref, s_ref)

    @pl.when(pl.program_id(0) == OWN // CB - 1)
    def _():
        lane = lax.broadcasted_iota(jnp.int32, (EOUT, 128), 1)
        packed = totals[0, :, COLS:]
        for i in range(3):
            t_ref[i * EOUT : (i + 1) * EOUT] = totals[i, :, 0:COLS]
            if i:
                packed = jnp.where(lane < 24 * i, packed, pltpu.roll(totals[i, :, COLS:], 24 * i, 1))
        t_ref[3 * EOUT :] = jnp.concatenate([packed[0 : EOUT // 2], packed[EOUT // 2 :]], 1)


def band_factors(where_ref, t_ref, u_ref, w_ref, re_ref, ro_ref, ce_ref, co_ref, f_ref):
    packed = t_ref[3 * EOUT :] + u_ref[3 * EOUT :]
    packed = jnp.concatenate([packed[:, 0:128], packed[:, 128:256]], 0)
    for i in range(3):
        slot = OWN + i
        group, k = slot // PER, slot % PER
        right, left = sorted_pair(where_ref[4], ce_ref[group], co_ref[group])
        below, above = sorted_pair(where_ref[3], re_ref[slot], ro_ref[slot])
        side = halo_tile(right, left, k)
        side = jnp.concatenate([side[0:72], side[88:96]], 0)
        weight = jnp.concatenate([w_ref[i], below[0:8], above[8:16]], 0)
        weight = jnp.concatenate([weight, side], 1)
        level = band_levels[i] * weight
        rows = slice(i * EOUT, (i + 1) * EOUT)
        outer = pltpu.roll(packed, 128 - 24 * i, 1) if i else packed
        total = jnp.concatenate([t_ref[rows] + u_ref[rows], outer], 1)
        f_ref[i] = level * lax.rsqrt(jnp.maximum(jnp.maximum(total, level * level), 1e-30))


def backward_kernel(where_ref, b_ref, t_ref, u_ref, w_ref, re_ref, ro_ref, ce_ref, co_ref,
                    cols_ref, rows_ref, out_ref, f_ref, s_ref, e1_ref, e2_ref):
    @pl.when(pl.program_id(0) == 0)
    def _():
        band_factors(where_ref, t_ref, u_ref, w_ref, re_ref, ro_ref, ce_ref, co_ref, f_ref)
        doubled(cols_ref.at[0], 0, e1_ref)
        doubled(cols_ref.at[0], WIDE, e2_ref)

    for j in range(CB):
        d0 = b_ref[j, 0] * f_ref[0]
        d1 = b_ref[j, 1] * f_ref[1]
        d2 = b_ref[j, 2] * f_ref[2]
        rows = slice(j * EOUT, (j + 1) * EOUT)
        for i, diff in enumerate((d1 - d0, d2 - d1)):
            high, low = split(diff)
            s_ref[i, rows, 0:WIDE] = high
            s_ref[i, rows, WIDE:] = low
        out_ref[j] = d0[0:ROWS, 0:COLS]
    r1 = rows_ref[0, 2 * WIDE : 2 * WIDE + ROWS, 0 : 2 * EOUT]
    r2 = rows_ref[0, 2 * WIDE + ROWS :, 0 : 2 * EOUT]
    y1 = mm(s_ref[0], e1_ref[...])
    y2 = mm(s_ref[1], e2_ref[...])
    for j in range(CB):
        rows = slice(j * EOUT, (j + 1) * EOUT)
        high, low = split(y1[rows])
        z = mm(r1, jnp.concatenate([high, low], 0))
        high, low = split(y2[rows])
        z += mm(r2, jnp.concatenate([high, low], 0))
        out_ref[j] += z


def rotation(gap, cross2, least):
    cross4 = cross2 * cross2
    square = gap * gap + (cross4 + 1e-37)
    root = square * lax.rsqrt(square) + tiny_value * GRAM_SCALE
    base = jnp.abs(gap) + root
    inverse = lax.rsqrt(base * base + cross4)
    signed = jnp.where(gap >= least, cross2, -cross2)
    return base * inverse, signed * inverse


def rotations(top, bottom, cross, least):
    both = [rotation(b - t, x + x, e) for t, b, x, e in zip(top, bottom, cross, least)]
    return tuple(p[0] for p in both), tuple(p[1] for p in both)


def shift(top, bottom):
    sub = lax.broadcasted_iota(jnp.int32, (8, 128), 0)
    (ta, tb), (ba, bb) = top, bottom
    down_a, down_b, first_b = pltpu.roll(ta, 1, 0), pltpu.roll(tb, 1, 0), pltpu.roll(ba, 1, 0)
    up_a, up_b = pltpu.roll(ba, 7, 0), pltpu.roll(bb, 7, 0)
    return (
        (jnp.where(sub == 0, ta, jnp.where(sub == 1, first_b, down_a)), jnp.where(sub == 0, down_a, down_b)),
        (jnp.where(sub == 7, up_b, up_a), jnp.where(sub == 7, tb, up_b)),
    )


def turn(cosine, sine, top, bottom):
    return shift(
        tuple(c * t - s * b for c, s, t, b in zip(cosine, sine, top, bottom)),
        tuple(s * t + c * b for c, s, t, b in zip(cosine, sine, top, bottom)),
    )


def dots(left, right):
    return [jnp.broadcast_to(jnp.sum(a * b, 1, keepdims=True), (8, 128)) for a, b in zip(left, right)]


def one_round(state, least):
    kt, kb, ut, ub = state
    c, s = rotations(dots(kt, ut), dots(kb, ub), dots(kt, ub), least)
    return turn(c, s, kt, kb) + turn(c, s, ut, ub)


def two_rounds(state, least, least_next):
    kt, kb, ut, ub = state
    top, bottom, cross = dots(kt, ut), dots(kb, ub), dots(kt, ub)
    kt_t, kb_t = shift(kt, kt)[0], shift(kb, kb)[0]
    ut_b, ub_b = shift(ut, ut)[1], shift(ub, ub)[1]
    quads = zip(dots(kt_t, ut_b), dots(kt_t, ub_b), dots(kb_t, ut_b), dots(kb_t, ub_b))
    c, s = rotations(top, bottom, cross, least)
    new_top, new_bottom = [], []
    for ci, si, t, b, x in zip(c, s, top, bottom, cross):
        cc, ss, mixed = ci * ci, si * si, (2.0 * ci * si) * x
        new_top.append(cc * t + ss * b - mixed)
        new_bottom.append(ss * t + cc * b + mixed)
    new_top, new_bottom = shift(new_top, new_bottom)
    of_t, of_b = shift(c, s), shift(tuple(-v for v in s), c)
    new_cross = [
        at * (ab * tt + bb * tb) + bt * (ab * bt_ + bb * bb_)
        for at, ab, bt, bb, (tt, tb, bt_, bb_) in zip(of_t[0], of_t[1], of_b[0], of_b[1], quads)
    ]
    c2, s2 = rotations(new_top, new_bottom, new_cross, least_next)
    kt, kb = turn(c2, s2, *turn(c, s, kt, kb))
    ut, ub = turn(c2, s2, *turn(c, s, ut, ub))
    return kt, kb, ut, ub


def jacobi_kernel(threshold, g_ref, h_ref, table, out_ref):
    lane = lax.broadcasted_iota(jnp.int32, (8, 128), 1)
    sub = lax.broadcasted_iota(jnp.int32, (8, 128), 0)
    gram = (g_ref[...] + h_ref[...]) * GRAM_SCALE
    rows = [gram[i : i + 1] for i in range(16)] + [gram[31 - i : 32 - i] for i in range(16)]
    k = [jnp.concatenate(rows[8 * i : 8 * i + 8], 0) for i in range(4)]
    u = [jnp.where(lane == label, 1.0, 0.0) for label in (sub, sub + 8, 31 - sub, 23 - sub)]
    state = ((k[0], k[1]), (k[2], k[3]), (u[0], u[1]), (u[2], u[3]))
    total = JSWEEPS * (ORDER - 1)

    def least(m):
        at = lax.rem(m, ORDER - 1)
        return table[at, 0:8], table[at, 8:16]

    state = lax.fori_loop(
        0, total // 2, lambda m, held: two_rounds(held, least(2 * m), least(2 * m + 1)), state
    )
    if total % 2:
        state = one_round(state, least(total - 1))
    kt, kb, ut, ub = state
    factors = []
    for value in dots(kt + kb, ut + ub):
        value = jnp.maximum(value * (1.0 / GRAM_SCALE), threshold * threshold)
        factors.append(1.0 - threshold / jnp.sqrt(value))
    vectors = jnp.concatenate(ut + ub, 0)
    mixing = lax.dot_general(
        jnp.concatenate(factors, 0) * vectors,
        vectors,
        (((0,), (0,)), ((), ())),
        precision=lax.Precision.HIGHEST,
        preferred_element_type=f32,
    )
    out_ref[...] = mixing[0:ORDER]


def apply_kernel(where_ref, m_ref, mine_ref, other_ref, near_ref, far1_ref, far2_ref, out_ref):
    chan = where_ref[2]
    own = m_ref[pl.ds(pl.multiple_of(chan * OWN, OWN), OWN), :]
    first = own[:, 0:16]
    second = own[:, 16:32]
    zero_chan = chan == 0
    mix = jnp.concatenate([jnp.where(zero_chan, first, second), jnp.where(zero_chan, second, first)], 1)
    high, low = split(mix)
    left = jnp.concatenate([high, high, low], 1)
    blank = jnp.zeros_like(left)
    left = jnp.concatenate([jnp.concatenate([left, blank], 1), jnp.concatenate([blank, left], 1)], 0)
    for own_ref, peer_ref, first_row, start, count in (
        (mine_ref, near_ref, 0, chan * 32, 32),
        (other_ref, near_ref.at[32:40], 0, (1 - chan) * 32, 8),
        (other_ref, far1_ref, 8, (1 - chan) * 32, 16),
        (other_ref, far2_ref, 24, (1 - chan) * 32, 8),
    ):
        for r in range(0, count, 8):
            pieces = []
            for j in range(0, 8, 2):
                stack = []
                for q in range(2):
                    both = jnp.concatenate([own_ref[first_row + r + j + q], peer_ref[r + j + q]], 0)
                    high, low = split(both)
                    stack += [high, low, high]
                pieces.append(mm(left, jnp.concatenate(stack, 0)).reshape(2, OWN, COLS))
            block = jnp.concatenate(pieces, 0)
            rows = pl.ds(pl.multiple_of(start + first_row + r, 8), 8)
            for c in range(2):
                out_ref[8 * c : 8 * c + 8, rows, :] = jnp.swapaxes(block[:, 8 * c : 8 * c + 8, :], 0, 1)


FORWARD, BACKWARD = stencil_tables()
LEAST = jacobi_tables()


def whole(shape):
    return pl.BlockSpec(shape, lambda i, where, n=len(shape): (0,) * n)


def at_place(table, axis):
    return pl.BlockSpec((1, *table.shape[1:]), lambda i, where: (where[axis], 0, 0))


def call(kernel, name, where, args, outs, specs=None, out_specs=None, scratch=(), grid=1, vmem=24, us=1.0):
    specs = specs or (None,) * len(args)
    out_specs = out_specs or (None,) * len(outs)
    return pl.pallas_call(
        kernel,
        out_shape=[jax.ShapeDtypeStruct(s, f32) for s in outs],
        grid_spec=pltpu.PrefetchScalarGridSpec(
            num_scalar_prefetch=1,
            grid=(grid,),
            in_specs=[whole(a.shape) if s is None else s for a, s in zip(args, specs)],
            out_specs=[whole(a) if s is None else s for a, s in zip(outs, out_specs)],
            scratch_shapes=list(scratch),
        ),
        compiler_params=pltpu.CompilerParams(vmem_limit_bytes=vmem * 2**20),
        cost_estimate=pl.CostEstimate(flops=0, bytes_accessed=int(us * 3.5e6), transcendentals=0),
        name=name,
    )(where, *args)


def shards(x, w):
    frow, fcol, chan = (lax.axis_index(a) for a in ("frow", "fcol", "chan"))
    last_r, last_c = lax.axis_size("frow") - 1, lax.axis_size("fcol") - 1

    def place(i, last):
        return jnp.where(i == 0, 0, jnp.where(i == last, 2, 1))

    where = jnp.stack([place(frow, last_r), place(fcol, last_c), chan, frow % 2, fcol % 2]).astype(jnp.int32)
    even = [(i, i ^ 1) for i in range(8)]
    odd = [(i, i + 1) for i in range(1, 7, 2)] + [(i + 1, i) for i in range(1, 7, 2)]
    swap = [(0, 1), (1, 0)]
    tile = (2, EIN, 128)
    half = (32, OWN, COLS)
    rim = (OWN + 3, 16, COLS)
    hbm = pl.BlockSpec(memory_space=pltpu.HBM)
    cut, rim_e, rim_o = call(
        cut_kernel,
        "cut",
        where,
        (x, w),
        ((OWN, 40, COLS), rim, rim),
        (hbm, hbm),
        scratch=(pltpu.SemaphoreType.DMA((6,)),),
        vmem=VFIRST,
    )
    near = lax.ppermute(cut, "chan", swap)
    rows_o = lax.ppermute(rim_o, "frow", odd)
    rows_e = lax.ppermute(rim_e, "frow", even)
    late, _ = lax.optimization_barrier((where, cut))
    side_e, side_o, mine, other = call(
        pack_kernel,
        "pack",
        late,
        (x, w),
        (tile, tile, half, half),
        (hbm, hbm),
        scratch=(pltpu.VMEM((OWN + 3, ROWS, COLS), f32), pltpu.SemaphoreType.DMA((5,))),
        us=1.5,
    )
    side_e, side_o = call(
        pack_halo_kernel, "pack_halo", where, (side_e, side_o, rows_e, rows_o), (tile, tile), us=0.7
    )
    cols_o = lax.ppermute(side_o, "fcol", odd)
    own, _ = lax.optimization_barrier((mine, side_o))
    send, near = call(gram_kernel, "gram", where, (own, near), ((ORDER, 128), (40, OWN, COLS)), us=1.2)
    side_e, _ = lax.optimization_barrier((side_e, send))
    cols_e = lax.ppermute(side_e, "fcol", even)
    got = lax.ppermute(send, "chan", swap)
    cols_e, cols_o, got = lax.optimization_barrier((cols_e, cols_o, got))
    steps = OWN // CB
    bands, totals = call(
        forward_steps,
        "forward",
        where,
        (x, rows_e, rows_o, cols_e, cols_o, FORWARD, FORWARD),
        ((OWN, 3, EOUT, WIDE), (3 * EOUT + EOUT // 2, COLS)),
        (None,) * 5 + (at_place(FORWARD, 1), at_place(FORWARD, 0)),
        (pl.BlockSpec((CB, 3, EOUT, WIDE), lambda i, where: (i, 0, 0, 0)), None),
        (
            pltpu.VMEM((CB, EOUT, WIDE), f32),
            pltpu.VMEM((2, CB * EOUT, 2 * WIDE), bf16),
            pltpu.VMEM((3, EOUT, WIDE), f32),
            pltpu.VMEM((2 * WIDE, WIDE), bf16),
            pltpu.VMEM((2 * WIDE, WIDE), bf16),
        ),
        steps,
        us=4.5,
    )
    totals_peer = lax.ppermute(totals, "chan", swap)
    part1, part2, _ = lax.optimization_barrier((mine[8:24], mine[24:32], totals))
    far1 = lax.ppermute(part1, "chan", swap)
    far2 = lax.ppermute(part2, "chan", swap)
    threshold = rank_level * math.sqrt(ROWS * COLS)
    send, _ = lax.optimization_barrier((send, totals))
    (mixing,) = call(
        lambda where_ref, *refs: jacobi_kernel(threshold, *refs),
        "jacobi",
        where,
        (send, got, LEAST),
        ((ORDER, 128),),
        us=8.5,
    )
    (back,) = call(
        backward_kernel,
        "backward",
        where,
        (bands, totals, totals_peer, w, rows_e, rows_o, cols_e, cols_o, BACKWARD, BACKWARD),
        ((OWN, ROWS, COLS),),
        (pl.BlockSpec((CB, 3, EOUT, WIDE), lambda i, where: (i, 0, 0, 0)),)
        + (None,) * 7
        + (at_place(BACKWARD, 1), at_place(BACKWARD, 0)),
        (pl.BlockSpec((CB, ROWS, COLS), lambda i, where: (i, 0, 0)),),
        (
            pltpu.VMEM((3, EOUT, WIDE), f32),
            pltpu.VMEM((2, CB * EOUT, 2 * WIDE), bf16),
            pltpu.VMEM((2 * WIDE, COLS), bf16),
            pltpu.VMEM((2 * WIDE, COLS), bf16),
        ),
        steps,
        us=4.5,
    )
    mixing, back = lax.optimization_barrier((mixing, back))
    (low,) = call(
        apply_kernel, "apply", where, (mixing, mine, other, near, far1, far2), ((OWN, ROWS, COLS),), us=2.4
    )
    return back, low


def solution(mesh):
    return jax.shard_map(
        shards,
        mesh=mesh,
        in_specs=(P("chan", "frow", "fcol"), P(None, "frow", "fcol")),
        out_specs=(P("chan", "frow", "fcol"), P("chan", "frow", "fcol")),
        check_vma=False,
    )
```

time: 83.1 us -> 50.2 us (0.60)
  the two profiles are of different devices: /device:TPU:25 before, /device:TPU:116 now
where the time goes in v2:
time: 50.2 us; the launch traced here: 50 us
  Pallas kernels  22.2 us (44%)
  starting transfers between devices  15.1 us (30%)
  waiting for transfers between devices  9.6 us (19%)
  local copies, waits for them, and re-layouts  2.29 us (5%)
  between operations  0.79 us (2%)
    pallas_call x8, Pallas kernels, call(): pl.pallas_call(kernel, out_shape=[jax.ShapeDtypeStruct(s, f32) for s in o...  22.2 us
    ppermute x1, waiting for transfers between devices, shards(): rows_o = lax.ppermute(rim_o, 'frow', odd)  4.11 us
    ppermute x1, waiting for transfers between devices, shards(): near = lax.ppermute(cut, 'chan', swap)  3.76 us
    ppermute x1, starting transfers between devices, shards(): cols_o = lax.ppermute(side_o, 'fcol', odd)  2.44 us
    ppermute x1, starting transfers between devices, shards(): rows_o = lax.ppermute(rim_o, 'frow', odd)  2.41 us
    ppermute x1, starting transfers between devices, shards(): cols_e = lax.ppermute(side_e, 'fcol', even)  2.34 us
    ppermute x1, starting transfers between devices, shards(): got = lax.ppermute(send, 'chan', swap)  2.32 us
    unnamed x14, local copies, waits for them, and re-layouts  2.18 us
  transfers between devices with their start and end apart: 9, of which 3 were waited for; matrix products, arithmetic and copies ran while one was open for 0% of the time, Pallas kernels for 30%

profile of v2, /device:TPU:116, one launch (start us, length us, event | category | flops | bytes accessed | tf_op | source)
XLA Modules:
  0.0 50.0 jit_solution(16831781231458363488)
XLA Ops:
  0.7 0.1 stack.23.where_ref
  0.7 1.2 %copy-done = f32[16,64,256]{2,1,0:T(8,128)S(1)} copy-done((f32[16,64,256]{2,1,0:T(8,128)S(1)}, f32[16,64,256]{2,1,0:T(8,128)}, u32[]{:S(2)}) %copy-start) | copy-done | bytes 1048600
  2.0 0.9 %copy-done.4 = f32[3,64,256]{2,1,0:T(8,128)S(1)} copy-done((f32[3,64,256]{2,1,0:T(8,128)S(1)}, f32[3,64,256]{2,1,0:T(8,128)}, u32[]{:S(2)}) %copy-start.4) | copy-done | bytes 196632
  2.9 0.7 %cut.1 = (f32[16,40,256]{2,1,0:T(8,128)S(1)}, f32[19,16,256]{2,1,0:T(8,128)S(1)}, f32[19,16,256]{2,1,0:T(8,128)S(1)}) custom-call(s32[5]{0:T(128)S(1)} %stack.23.where_ref, f32[16,64,256]{2,1,0:T(8,128)S(1)} %copy-done, f32[3,64,256]{2,1,0:T(8,128)S(1)} %copy-done.4), custom_call_target="tpu_custom_call" | custom-call | bytes 3500000 | tf_op jit(solution)/shard_map/cut/pallas_call | solution.py:470
  3.7 1.4 %collective-permute-start.2 = (f32[16,40,256]{2,1,0:T(8,128)S(1)}, f32[16,40,256]{2,1,0:T(8,128)S(1)}, u32[]{:S(2)}, u32[]{:S(2)}) collective-permute-start(f32[16,40,256]{2,1,0:T(8,128)S(1)} %get-tuple-element.26), channel_id=1, source_target_pairs={{0,1},{1,0},{2,3},{3,2},{4,5},{5,4},{6,7},{7,6},{8,9},{9,8},{10,11... | collective-permute-start | bytes 1966088 | tf_op jit(solution)/shard_map/ppermute | solution.py:511
  5.0 2.4 %collective-permute-start.1 = (f32[19,16,256]{2,1,0:T(8,128)S(1)}, f32[19,16,256]{2,1,0:T(8,128)S(1)}, u32[]{:S(2)}, u32[]{:S(2)}) collective-permute-start(f32[19,16,256]{2,1,0:T(8,128)S(1)} %get-tuple-element.32), channel_id=1, source_target_pairs={{16,32},{48,64},{80,96},{32,16},{64,48},{96,80},{17,33},{49,65},{8... | collective-permute-start | bytes 933896 | tf_op jit(solution)/shard_map/ppermute | solution.py:512
  7.4 1.7 %pack.1 = (f32[2,96,128]{2,1,0:T(8,128)S(1)}, f32[2,96,128]{2,1,0:T(8,128)S(1)}, f32[32,16,256]{2,1,0:T(8,128)S(1)}, f32[32,16,256]{2,1,0:T(8,128)S(1)}) custom-call(s32[5]{0:T(128)S(1)} %stack.23.where_ref, f32[16,64,256]{2,1,0:T(8,128)S(1)} %copy-done, f32[3,64,256]{2,1,0:T(8,128)S(1)} %copy-done.4), custom_call_target="tpu_custom_call" | custom-call | bytes 5250000 | tf_op jit(solution)/shard_map/pack/pallas_call | solution.py:470
  9.1 4.1 %collective-permute-done.1.rows_o.ro_ref = f32[19,16,256]{2,1,0:T(8,128)S(1)} collective-permute-done((f32[19,16,256]{2,1,0:T(8,128)S(1)}, f32[19,16,256]{2,1,0:T(8,128)S(1)}, u32[]{:S(2)}, u32[]{:S(2)}) %collective-permute-start.1) | collective-permute-done | bytes 311328 | tf_op jit(solution)/shard_map/ppermute | solution.py:512
  13.2 0.8 %pack_halo.1 = (f32[2,96,128]{2,1,0:T(8,128)S(1)}, f32[2,96,128]{2,1,0:T(8,128)S(1)}) custom-call(s32[5]{0:T(128)S(1)} %stack.23.where_ref, f32[2,96,128]{2,1,0:T(8,128)S(1)} %get-tuple-element.29.old_e, f32[2,96,128]{2,1,0:T(8,128)S(1)} %get-tuple-element.30.old_o, f32[19,16,256]{2,1,0:T(8,128)S(1)} %collective-permute-done.rows_e.re_ref, ...), custom_call_target="tpu_custom_call" | custom-call | bytes 2450000 | tf_op jit(solution)/shard_map/pack_halo/pallas_call | solution.py:470
  14.0 2.4 %collective-permute-start.4 = (f32[2,96,128]{2,1,0:T(8,128)S(1)}, f32[2,96,128]{2,1,0:T(8,128)S(1)}, u32[]{:S(2)}, u32[]{:S(2)}) collective-permute-start(f32[2,96,128]{2,1,0:T(8,128)S(1)} %get-tuple-element.33), channel_id=1, source_target_pairs={{2,4},{6,8},{10,12},{4,2},{8,6},{12,10},{3,5},{7,9},{11,13},{5,3},... | collective-permute-start | bytes 294920 | tf_op jit(solution)/shard_map/ppermute | solution.py:528
  16.4 3.8 %collective-permute-done.2.peer_ref = f32[16,40,256]{2,1,0:T(8,128)S(1)} collective-permute-done((f32[16,40,256]{2,1,0:T(8,128)S(1)}, f32[16,40,256]{2,1,0:T(8,128)S(1)}, u32[]{:S(2)}, u32[]{:S(2)}) %collective-permute-start.2) | collective-permute-done | bytes 655392 | tf_op jit(solution)/shard_map/ppermute | solution.py:511
  20.2 1.2 %gram.1 = (f32[32,128]{1,0:T(8,128)S(1)}, f32[40,16,256]{2,1,0:T(8,128)S(1)}) custom-call(s32[5]{0:T(128)S(1)} %stack.23.where_ref, f32[32,16,256]{2,1,0:T(8,128)S(1)} %get-tuple-element.34.own_ref.mine_ref, f32[16,40,256]{2,1,0:T(8,128)S(1)} %collective-permute-done.2.peer_ref), custom_call_target="tpu_custom_call" | custom-call | bytes 4200000 | tf_op jit(solution)/shard_map/gram/pallas_call | solution.py:470
  21.4 0.0 copy-start.3
  21.4 0.0 copy-start.5
  21.4 2.3 %collective-permute-start.3 = (f32[2,96,128]{2,1,0:T(8,128)S(1)}, f32[2,96,128]{2,1,0:T(8,128)S(1)}, u32[]{:S(2)}, u32[]{:S(2)}) collective-permute-start(f32[2,96,128]{2,1,0:T(8,128)S(1)} %get-tuple-element.37), channel_id=1, source_target_pairs={{0,2},{2,0},{4,6},{6,4},{8,10},{10,8},{12,14},{14,12},{1,3},{3,1},... | collective-permute-start | bytes 294920 | tf_op jit(solution)/shard_map/ppermute | solution.py:532
  23.8 2.3 %collective-permute-start.5 = (f32[32,128]{1,0:T(8,128)S(1)}, f32[32,128]{1,0:T(8,128)S(1)}, u32[]{:S(2)}, u32[]{:S(2)}) collective-permute-start(f32[32,128]{1,0:T(8,128)S(1)} %get-tuple-element.41.refs_0_), channel_id=1, source_target_pairs={{0,1},{1,0},{2,3},{3,2},{4,5},{5,4},{6,7},{7,6},{8,9},{9,8},{10,11... | collective-permute-start | bytes 49160 | tf_op jit(solution)/shard_map/ppermute | solution.py:533
  26.1 1.7 %collective-permute-done.5.refs_1_ = f32[32,128]{1,0:T(8,128)S(1)} collective-permute-done((f32[32,128]{1,0:T(8,128)S(1)}, f32[32,128]{1,0:T(8,128)S(1)}, u32[]{:S(2)}, u32[]{:S(2)}) %collective-permute-start.5) | collective-permute-done | bytes 16416 | tf_op jit(solution)/shard_map/ppermute | solution.py:533
  27.8 4.0 %forward.1 = (f32[16,3,80,384]{3,2,1,0:T(8,128)S(1)}, f32[280,256]{1,0:T(8,128)S(1)}) custom-call(s32[5]{0:T(128)S(1)} %stack.23.where_ref, f32[16,64,256]{2,1,0:T(8,128)S(1)} %copy-done.1, f32[19,16,256]{2,1,0:T(8,128)S(1)} %collective-permute-done.rows_e.re_ref, f32[19,16,256]{2,1,0:T(8,128)S(1)} %collective-permute-done.1.rows_o.ro_ref, ...), custom_call_target="tpu_custom_call" | custom-call | bytes 15750000 | tf_op jit(solution)/shard_map/forward/pallas_call | solution.py:470
  31.9 2.1 %collective-permute-start.6 = (f32[280,256]{1,0:T(8,128)S(1)}, f32[280,256]{1,0:T(8,128)S(1)}, u32[]{:S(2)}, u32[]{:S(2)}) collective-permute-start(f32[280,256]{1,0:T(8,128)S(1)} %get-tuple-element.40.t_ref), channel_id=1, source_target_pairs={{0,1},{1,0},{2,3},{3,2},{4,5},{5,4},{6,7},{7,6},{8,9},{9,8},{10,11... | collective-permute-start | bytes 860168 | tf_op jit(solution)/shard_map/ppermute | solution.py:554
  34.0 0.1 collective-permute-start.7
  34.1 2.0 %collective-permute-start.8 = (f32[8,16,256]{2,1,0:T(8,128)S(1)}, f32[8,16,256]{2,1,0:T(8,128)S(1)}, u32[]{:S(2)}, u32[]{:S(2)}) collective-permute-start(f32[8,16,256]{2,1,0:T(8,128)S(1)} %slice.7), channel_id=1, source_target_pairs={{0,1},{1,0},{2,3},{3,2},{4,5},{5,4},{6,7},{7,6},{8,9},{9,8},{10,11... | collective-permute-start | bytes 393224 | tf_op jit(solution)/shard_map/ppermute | solution.py:557
  36.1 7.6 %jacobi.1.m_ref = f32[32,128]{1,0:T(8,128)S(1)} custom-call(s32[5]{0:T(128)S(1)} %stack.23.where_ref, f32[32,128]{1,0:T(8,128)S(1)} %get-tuple-element.41.refs_0_, f32[32,128]{1,0:T(8,128)S(1)} %collective-permute-done.5.refs_1_, f32[31,16,128]{2,1,0:T(8,128)S(1)} %copy-done.6), custom_call_target="tpu_custom_call" | custom-call | bytes 29750000 | tf_op jit(solution)/shard_map/jacobi/pallas_call | solution.py:470
  43.7 3.9 %backward.1 = f32[16,64,256]{2,1,0:T(8,128)} custom-call(s32[5]{0:T(128)S(1)} %stack.23.where_ref, f32[16,3,80,384]{3,2,1,0:T(8,128)S(1)} %get-tuple-element.43.b_ref, f32[280,256]{1,0:T(8,128)S(1)} %get-tuple-element.40.t_ref, f32[280,256]{1,0:T(8,128)S(1)} %collective-permute-done.6.u_ref, f32[3,64,256]{2,1,0:T(8,128)S(1)} %copy-done.5, ...), custom_call_target="tpu_custom_call" | custom-call | bytes 15750000 | tf_op jit(solution)/shard_map/backward/pallas_call | solution.py:470
  47.6 2.4 %apply.1 = f32[16,64,256]{2,1,0:T(8,128)} custom-call(s32[5]{0:T(128)S(1)} %stack.23.where_ref, f32[32,128]{1,0:T(8,128)S(1)} %jacobi.1.m_ref, f32[32,16,256]{2,1,0:T(8,128)S(1)} %get-tuple-element.34.own_ref.mine_ref, f32[32,16,256]{2,1,0:T(8,128)S(1)} %get-tuple-element.46.other_ref, f32[40,16,256]{2,1,0:T(8,128)S(1)} %get-tuple-element.47.near_ref, ...), custom_call_target="tpu_custom_call" | custom-call | bytes 8400000 | tf_op jit(solution)/shard_map/apply/pallas_call | solution.py:470
  (19 shorter events, 0.1 us)
Async XLA Ops:
  0.7 1.2 %copy-start = (f32[16,64,256]{2,1,0:T(8,128)S(1)}, f32[16,64,256]{2,1,0:T(8,128)}, u32[]{:S(2)}) copy-start(f32[16,64,256]{2,1,0:T(8,128)} %x_ref.5) | copy-start | bytes 3145732
  2.0 0.9 %copy-start.4 = (f32[3,64,256]{2,1,0:T(8,128)S(1)}, f32[3,64,256]{2,1,0:T(8,128)}, u32[]{:S(2)}) copy-start(f32[3,64,256]{2,1,0:T(8,128)} %w_ref.5) | copy-start | bytes 589828
  2.9 24.9 %copy-start.1 = (f32[16,64,256]{2,1,0:T(8,128)S(1)}, f32[16,64,256]{2,1,0:T(8,128)}, u32[]{:S(2)}) copy-start(f32[16,64,256]{2,1,0:T(8,128)} %x_ref.5) | copy-start | bytes 3145732
  2.9 24.9 %copy-start.2 = (bf16[3,928,384]{2,1,0:T(8,128)(2,1)S(1)}, bf16[3,928,384]{2,1,0:T(8,128)(2,1)}, u32[]{:S(2)}) copy-start(bf16[3,928,384]{2,1,0:T(8,128)(2,1)} %constant.39.clone.cols_ref.rows_ref) | copy-start | bytes 6414340
  3.7 16.6 %collective-permute-start.2 = (f32[16,40,256]{2,1,0:T(8,128)S(1)}, f32[16,40,256]{2,1,0:T(8,128)S(1)}, u32[]{:S(2)}, u32[]{:S(2)}) collective-permute-start(f32[16,40,256]{2,1,0:T(8,128)S(1)} %get-tuple-element.26), channel_id=1, source_target_pairs={{0,1},{1,0},{2,3},{3,2},{4,5},{5,4},{6,7},{7,6},{8,9},{9,8},{10,11... | collective-permute-start | bytes 1966088 | tf_op jit(solution)/shard_map/ppermute | solution.py:511
  5.0 4.1 %collective-permute-start = (f32[19,16,256]{2,1,0:T(8,128)S(1)}, f32[19,16,256]{2,1,0:T(8,128)S(1)}, u32[]{:S(2)}, u32[]{:S(2)}) collective-permute-start(f32[19,16,256]{2,1,0:T(8,128)S(1)} %get-tuple-element.31), channel_id=1, source_target_pairs={{0,16},{16,0},{32,48},{48,32},{64,80},{80,64},{96,112},{112,96},{1... | collective-permute-start | bytes 933896 | tf_op jit(solution)/shard_map/ppermute | solution.py:513
  5.0 8.2 %collective-permute-start.1 = (f32[19,16,256]{2,1,0:T(8,128)S(1)}, f32[19,16,256]{2,1,0:T(8,128)S(1)}, u32[]{:S(2)}, u32[]{:S(2)}) collective-permute-start(f32[19,16,256]{2,1,0:T(8,128)S(1)} %get-tuple-element.32), channel_id=1, source_target_pairs={{16,32},{48,64},{80,96},{32,16},{64,48},{96,80},{17,33},{49,65},{8... | collective-permute-start | bytes 933896 | tf_op jit(solution)/shard_map/ppermute | solution.py:512
  14.0 12.1 %collective-permute-start.4 = (f32[2,96,128]{2,1,0:T(8,128)S(1)}, f32[2,96,128]{2,1,0:T(8,128)S(1)}, u32[]{:S(2)}, u32[]{:S(2)}) collective-permute-start(f32[2,96,128]{2,1,0:T(8,128)S(1)} %get-tuple-element.33), channel_id=1, source_target_pairs={{2,4},{6,8},{10,12},{4,2},{8,6},{12,10},{3,5},{7,9},{11,13},{5,3},... | collective-permute-start | bytes 294920 | tf_op jit(solution)/shard_map/ppermute | solution.py:528
  21.4 14.7 %copy-start.6 = (f32[31,16,128]{2,1,0:T(8,128)S(1)}, f32[31,16,128]{2,1,0:T(8,128)}, u32[]{:S(2)}) copy-start(f32[31,16,128]{2,1,0:T(8,128)} %constant.40.clone.refs_2_) | copy-start | bytes 761860
  21.4 22.3 %copy-start.3 = (bf16[3,896,256]{2,1,0:T(8,128)(2,1)S(1)}, bf16[3,896,256]{2,1,0:T(8,128)(2,1)}, u32[]{:S(2)}) copy-start(bf16[3,896,256]{2,1,0:T(8,128)(2,1)} %constant.41.clone.cols_ref.rows_ref) | copy-start | bytes 4128772
  21.4 22.3 %copy-start.5 = (f32[3,64,256]{2,1,0:T(8,128)S(1)}, f32[3,64,256]{2,1,0:T(8,128)}, u32[]{:S(2)}) copy-start(f32[3,64,256]{2,1,0:T(8,128)} %w_ref.5) | copy-start | bytes 589828
  21.4 6.4 %collective-permute-start.3 = (f32[2,96,128]{2,1,0:T(8,128)S(1)}, f32[2,96,128]{2,1,0:T(8,128)S(1)}, u32[]{:S(2)}, u32[]{:S(2)}) collective-permute-start(f32[2,96,128]{2,1,0:T(8,128)S(1)} %get-tuple-element.37), channel_id=1, source_target_pairs={{0,2},{2,0},{4,6},{6,4},{8,10},{10,8},{12,14},{14,12},{1,3},{3,1},... | collective-permute-start | bytes 294920 | tf_op jit(solution)/shard_map/ppermute | solution.py:532
  23.8 4.0 %collective-permute-start.5 = (f32[32,128]{1,0:T(8,128)S(1)}, f32[32,128]{1,0:T(8,128)S(1)}, u32[]{:S(2)}, u32[]{:S(2)}) collective-permute-start(f32[32,128]{1,0:T(8,128)S(1)} %get-tuple-element.41.refs_0_), channel_id=1, source_target_pairs={{0,1},{1,0},{2,3},{3,2},{4,5},{5,4},{6,7},{7,6},{8,9},{9,8},{10,11... | collective-permute-start | bytes 49160 | tf_op jit(solution)/shard_map/ppermute | solution.py:533
  31.9 11.8 %collective-permute-start.6 = (f32[280,256]{1,0:T(8,128)S(1)}, f32[280,256]{1,0:T(8,128)S(1)}, u32[]{:S(2)}, u32[]{:S(2)}) collective-permute-start(f32[280,256]{1,0:T(8,128)S(1)} %get-tuple-element.40.t_ref), channel_id=1, source_target_pairs={{0,1},{1,0},{2,3},{3,2},{4,5},{5,4},{6,7},{7,6},{8,9},{9,8},{10,11... | collective-permute-start | bytes 860168 | tf_op jit(solution)/shard_map/ppermute | solution.py:554
  34.0 13.6 %collective-permute-start.7 = (f32[16,16,256]{2,1,0:T(8,128)S(1)}, f32[16,16,256]{2,1,0:T(8,128)S(1)}, u32[]{:S(2)}, u32[]{:S(2)}) collective-permute-start(f32[16,16,256]{2,1,0:T(8,128)S(1)} %slice.6), channel_id=1, source_target_pairs={{0,1},{1,0},{2,3},{3,2},{4,5},{5,4},{6,7},{7,6},{8,9},{9,8},{10,11... | collective-permute-start | bytes 786440 | tf_op jit(solution)/shard_map/ppermute | solution.py:556
  34.1 13.5 %collective-permute-start.8 = (f32[8,16,256]{2,1,0:T(8,128)S(1)}, f32[8,16,256]{2,1,0:T(8,128)S(1)}, u32[]{:S(2)}, u32[]{:S(2)}) collective-permute-start(f32[8,16,256]{2,1,0:T(8,128)S(1)} %slice.7), channel_id=1, source_target_pairs={{0,1},{1,0},{2,3},{3,2},{4,5},{5,4},{6,7},{7,6},{8,9},{9,8},{10,11... | collective-permute-start | bytes 393224 | tf_op jit(solution)/shard_map/ppermute | solution.py:557

commit v3 on v2

--- a/solution.py
+++ b/solution.py
@@ -26,7 +26,6 @@
 EIN, EOUT = 96, 80
 WIDE = 384
 GRAM_SCALE = float(2.0**32)
-VFIRST = 24
 CB = 8
 
 
@@ -101,22 +100,31 @@
     return jnp.dot(a, b, preferred_element_type=f32)
 
 
-def cut_kernel(where_ref, x_ref, w_ref, half_ref, even_ref, odd_ref, sems):
+def cut_kernel(where_ref, x_ref, half_ref, sems):
     start = pl.multiple_of((1 - where_ref[2]) * 32, 32)
     own = pl.multiple_of(where_ref[2] * 32, 32)
     copies = [
         (x_ref.at[:, pl.ds(start, 32), :], half_ref.at[:, 0:32, :]),
         (x_ref.at[:, pl.ds(own, 8), :], half_ref.at[:, 32:40, :]),
     ]
-    for out_ref, parity in ((even_ref, 1 - where_ref[3]), (odd_ref, where_ref[3])):
-        rows = pl.ds(pl.multiple_of(parity * 48, 16), 16)
-        copies.append((x_ref.at[:, rows, :], out_ref.at[0:OWN]))
-        copies.append((w_ref.at[:, rows, :], out_ref.at[OWN : OWN + 3]))
+    copy_all(copies, sems)
+
+
+def copy_all(copies, sems):
     copies = [pltpu.make_async_copy(a, b, sems.at[i]) for i, (a, b) in enumerate(copies)]
     for copy in copies:
         copy.start()
     for copy in copies:
         copy.wait()
+
+
+def rim_kernel(where_ref, x_ref, w_ref, even_ref, odd_ref, sems):
+    copies = []
+    for out_ref, parity in ((even_ref, 1 - where_ref[3]), (odd_ref, where_ref[3])):
+        rows = pl.ds(pl.multiple_of(parity * 48, 16), 16)
+        copies.append((x_ref.at[:, rows, :], out_ref.at[0:OWN]))
+        copies.append((w_ref.at[:, rows, :], out_ref.at[OWN : OWN + 3]))
+    copy_all(copies, sems)
 
 
 def pack_rows(tiles, count, even_ref, odd_ref, at, parity):
@@ -420,36 +428,43 @@
     out_ref[...] = mixing[0:ORDER]
 
 
-def apply_kernel(where_ref, m_ref, mine_ref, other_ref, near_ref, far1_ref, far2_ref, out_ref):
-    chan = where_ref[2]
-    own = m_ref[pl.ds(pl.multiple_of(chan * OWN, OWN), OWN), :]
+def mixing_left(where_ref, m_ref):
+    own = m_ref[pl.ds(pl.multiple_of(where_ref[2] * OWN, OWN), OWN), :]
     first = own[:, 0:16]
     second = own[:, 16:32]
-    zero_chan = chan == 0
+    zero_chan = where_ref[2] == 0
     mix = jnp.concatenate([jnp.where(zero_chan, first, second), jnp.where(zero_chan, second, first)], 1)
     high, low = split(mix)
     left = jnp.concatenate([high, high, low], 1)
     blank = jnp.zeros_like(left)
-    left = jnp.concatenate([jnp.concatenate([left, blank], 1), jnp.concatenate([blank, left], 1)], 0)
-    for own_ref, peer_ref, first_row, start, count in (
-        (mine_ref, near_ref, 0, chan * 32, 32),
-        (other_ref, near_ref.at[32:40], 0, (1 - chan) * 32, 8),
-        (other_ref, far1_ref, 8, (1 - chan) * 32, 16),
-        (other_ref, far2_ref, 24, (1 - chan) * 32, 8),
-    ):
-        for r in range(0, count, 8):
-            pieces = []
-            for j in range(0, 8, 2):
-                stack = []
-                for q in range(2):
-                    both = jnp.concatenate([own_ref[first_row + r + j + q], peer_ref[r + j + q]], 0)
-                    high, low = split(both)
-                    stack += [high, low, high]
-                pieces.append(mm(left, jnp.concatenate(stack, 0)).reshape(2, OWN, COLS))
-            block = jnp.concatenate(pieces, 0)
-            rows = pl.ds(pl.multiple_of(start + first_row + r, 8), 8)
-            for c in range(2):
-                out_ref[8 * c : 8 * c + 8, rows, :] = jnp.swapaxes(block[:, 8 * c : 8 * c + 8, :], 0, 1)
+    return jnp.concatenate([jnp.concatenate([left, blank], 1), jnp.concatenate([blank, left], 1)], 0)
+
+
+def apply_rows(left, own_ref, peer_ref, out_ref, first_row, count):
+    for r in range(0, count, 8):
+        pieces = []
+        for j in range(0, 8, 2):
+            stack = []
+            for q in range(2):
+                both = jnp.concatenate([own_ref[first_row + r + j + q], peer_ref[r + j + q]], 0)
+                high, low = split(both)
+                stack += [high, low, high]
+            pieces.append(mm(left, jnp.concatenate(stack, 0)).reshape(2, OWN, COLS))
+        block = jnp.concatenate(pieces, 0)
+        for c in range(2):
+            rows = slice(first_row + r, first_row + r + 8)
+            out_ref[8 * c : 8 * c + 8, rows, :] = jnp.swapaxes(block[:, 8 * c : 8 * c + 8, :], 0, 1)
+
+
+def apply_near(where_ref, m_ref, mine_ref, near_ref, out_ref):
+    apply_rows(mixing_left(where_ref, m_ref), mine_ref, near_ref, out_ref, 0, 32)
+
+
+def apply_far(where_ref, m_ref, other_ref, near_ref, far1_ref, far2_ref, done_ref, out_ref):
+    left = mixing_left(where_ref, m_ref)
+    apply_rows(left, other_ref, near_ref.at[32:40], out_ref, 0, 8)
+    apply_rows(left, other_ref, far1_ref, out_ref, 8, 16)
+    apply_rows(left, other_ref, far2_ref, out_ref, 24, 8)
 
 
 FORWARD, BACKWARD = stencil_tables()
@@ -464,7 +479,7 @@
     return pl.BlockSpec((1, *table.shape[1:]), lambda i, where: (where[axis], 0, 0))
 
 
-def call(kernel, name, where, args, outs, specs=None, out_specs=None, scratch=(), grid=1, vmem=24, us=1.0):
+def call(kernel, name, where, args, outs, specs=None, out_specs=None, scratch=(), grid=1, vmem=24, us=1.0, alias=None):
     specs = specs or (None,) * len(args)
     out_specs = out_specs or (None,) * len(outs)
     return pl.pallas_call(
@@ -479,6 +494,7 @@
         ),
         compiler_params=pltpu.CompilerParams(vmem_limit_bytes=vmem * 2**20),
         cost_estimate=pl.CostEstimate(flops=0, bytes_accessed=int(us * 3.5e6), transcendentals=0),
+        input_output_aliases=alias or {},
         name=name,
     )(where, *args)
 
@@ -498,20 +514,17 @@
     half = (32, OWN, COLS)
     rim = (OWN + 3, 16, COLS)
     hbm = pl.BlockSpec(memory_space=pltpu.HBM)
-    cut, rim_e, rim_o = call(
-        cut_kernel,
-        "cut",
-        where,
-        (x, w),
-        ((OWN, 40, COLS), rim, rim),
-        (hbm, hbm),
-        scratch=(pltpu.SemaphoreType.DMA((6,)),),
-        vmem=VFIRST,
+    (cut,) = call(
+        cut_kernel, "cut", where, (x,), ((OWN, 40, COLS),), (hbm,), scratch=(pltpu.SemaphoreType.DMA((2,)),), us=0.6
     )
     near = lax.ppermute(cut, "chan", swap)
+    later, _ = lax.optimization_barrier((where, cut))
+    rim_e, rim_o = call(
+        rim_kernel, "rim", later, (x, w), (rim, rim), (hbm, hbm), scratch=(pltpu.SemaphoreType.DMA((4,)),), us=0.6
+    )
     rows_o = lax.ppermute(rim_o, "frow", odd)
     rows_e = lax.ppermute(rim_e, "frow", even)
-    late, _ = lax.optimization_barrier((where, cut))
+    late, _ = lax.optimization_barrier((where, rim_e))
     side_e, side_o, mine, other = call(
         pack_kernel,
         "pack",
@@ -565,6 +578,17 @@
         ((ORDER, 128),),
         us=8.5,
     )
+    (low,) = call(
+        apply_near,
+        "apply_near",
+        where,
+        (mixing, mine, near),
+        ((OWN, ROWS, COLS),),
+        None,
+        (pl.BlockSpec((OWN, 32, COLS), lambda i, where: (0, where[2], 0)),),
+        us=1.2,
+    )
+    totals_peer, low = lax.optimization_barrier((totals_peer, low))
     (back,) = call(
         backward_kernel,
         "backward",
@@ -584,9 +608,17 @@
         steps,
         us=4.5,
     )
-    mixing, back = lax.optimization_barrier((mixing, back))
+    low, back = lax.optimization_barrier((low, back))
     (low,) = call(
-        apply_kernel, "apply", where, (mixing, mine, other, near, far1, far2), ((OWN, ROWS, COLS),), us=2.4
+        apply_far,
+        "apply_far",
+        where,
+        (mixing, other, near, far1, far2, low),
+        ((OWN, ROWS, COLS),),
+        (None,) * 5 + (hbm,),
+        (pl.BlockSpec((OWN, 32, COLS), lambda i, where: (0, 1 - where[2], 0)),),
+        us=1.2,
+        alias={6: 0},
     )
     return back, low
 

time: 50.2 us -> 49.5 us (0.986)
  starting transfers between devices: 15.1 us -> 12.9 us
  Pallas kernels: 22.2 us -> 24.2 us
    pallas_call x8 -> x10, Pallas kernels: 22.2 us -> 24.2 us  [call(): pl.pallas_call(kernel, out_shape=[jax.ShapeDtypeStruct(s, f32) for s in o...]
    ppermute x1, waiting for transfers between devices: 3.76 us -> 2.15 us  [shards(): near = lax.ppermute(cut, 'chan', swap)]
    ppermute x1, starting transfers between devices: 2.32 us -> 1.28 us  [shards(): got = lax.ppermute(send, 'chan', swap)]
    ppermute x1, starting transfers between devices: 2.1 us -> 1.36 us  [shards(): totals_peer = lax.ppermute(totals, 'chan', swap)]
    ppermute x1, waiting for transfers between devices: 1.71 us -> 2.45 us  [shards(): got = lax.ppermute(send, 'chan', swap)]
    ppermute x1, starting transfers between devices: 0.1 us -> 0.82 us  [shards(): far1 = lax.ppermute(part1, 'chan', swap)]
    ppermute x1, starting transfers between devices: 2.01 us -> 1.28 us  [shards(): far2 = lax.ppermute(part2, 'chan', swap)]
  transfers between devices with their start and end apart: 9 -> 9, of which waited for: 3 -> 3; matrix products, arithmetic and copies ran while one was open for 0% -> 0% of each run, Pallas kernels for 30% -> 36%
where the time goes in v3:
time: 49.5 us; the launch traced here: 49.3 us
  Pallas kernels  24.2 us (49%)
  starting transfers between devices  12.9 us (26%)
  waiting for transfers between devices  9.15 us (18%)
  local copies, waits for them, and re-layouts  2.3 us (5%)
  between operations  0.8 us (2%)
    pallas_call x10, Pallas kernels, call(): pl.pallas_call(kernel, out_shape=[jax.ShapeDtypeStruct(s, f32) for s in o...  24.2 us
    ppermute x1, waiting for transfers between devices, shards(): rows_o = lax.ppermute(rim_o, 'frow', odd)  4.53 us
    ppermute x1, waiting for transfers between devices, shards(): got = lax.ppermute(send, 'chan', swap)  2.45 us
    ppermute x1, starting transfers between devices, shards(): cols_o = lax.ppermute(side_o, 'fcol', odd)  2.44 us
    ppermute x1, starting transfers between devices, shards(): cols_e = lax.ppermute(side_e, 'fcol', even)  2.32 us
    unnamed x14, local copies, waits for them, and re-layouts  2.18 us
    ppermute x1, waiting for transfers between devices, shards(): near = lax.ppermute(cut, 'chan', swap)  2.15 us
    ppermute x1, starting transfers between devices, shards(): rows_o = lax.ppermute(rim_o, 'frow', odd)  1.92 us
  transfers between devices with their start and end apart: 9, of which 3 were waited for; matrix products, arithmetic and copies ran while one was open for 0% of the time, Pallas kernels for 36%

profile of v3, /device:TPU:116, one launch (start us, length us, event | category | flops | bytes accessed | tf_op | source)
XLA Modules:
  0.0 49.3 jit_solution(15669429133897215454)
XLA Ops:
  0.7 0.1 stack.23.where_ref
  0.8 1.2 %copy-done = f32[16,64,256]{2,1,0:T(8,128)S(1)} copy-done((f32[16,64,256]{2,1,0:T(8,128)S(1)}, f32[16,64,256]{2,1,0:T(8,128)}, u32[]{:S(2)}) %copy-start) | copy-done | bytes 1048600
  2.0 0.6 %cut.1 = f32[16,40,256]{2,1,0:T(8,128)S(1)} custom-call(s32[5]{0:T(128)S(1)} %stack.23.where_ref, f32[16,64,256]{2,1,0:T(8,128)S(1)} %copy-done), custom_call_target="tpu_custom_call" | custom-call | bytes 2100000 | tf_op jit(solution)/shard_map/cut/pallas_call | solution.py:485
  2.6 1.4 %collective-permute-start.2 = (f32[16,40,256]{2,1,0:T(8,128)S(1)}, f32[16,40,256]{2,1,0:T(8,128)S(1)}, u32[]{:S(2)}, u32[]{:S(2)}) collective-permute-start(f32[16,40,256]{2,1,0:T(8,128)S(1)} %cut.1), channel_id=1, source_target_pairs={{0,1},{1,0},{2,3},{3,2},{4,5},{5,4},{6,7},{7,6},{8,9},{9,8},{10,11... | collective-permute-start | bytes 1966088 | tf_op jit(solution)/shard_map/ppermute | solution.py:520
  4.0 0.9 %copy-done.4 = f32[3,64,256]{2,1,0:T(8,128)S(1)} copy-done((f32[3,64,256]{2,1,0:T(8,128)S(1)}, f32[3,64,256]{2,1,0:T(8,128)}, u32[]{:S(2)}) %copy-start.4) | copy-done | bytes 196632
  4.9 0.7 %rim.1 = (f32[19,16,256]{2,1,0:T(8,128)S(1)}, f32[19,16,256]{2,1,0:T(8,128)S(1)}) custom-call(s32[5]{0:T(128)S(1)} %stack.23.where_ref, f32[16,64,256]{2,1,0:T(8,128)S(1)} %copy-done, f32[3,64,256]{2,1,0:T(8,128)S(1)} %copy-done.4), custom_call_target="tpu_custom_call" | custom-call | bytes 2100000 | tf_op jit(solution)/shard_map/rim/pallas_call | solution.py:485
  5.6 1.9 %collective-permute-start.1 = (f32[19,16,256]{2,1,0:T(8,128)S(1)}, f32[19,16,256]{2,1,0:T(8,128)S(1)}, u32[]{:S(2)}, u32[]{:S(2)}) collective-permute-start(f32[19,16,256]{2,1,0:T(8,128)S(1)} %get-tuple-element.30), channel_id=1, source_target_pairs={{16,32},{48,64},{80,96},{32,16},{64,48},{96,80},{17,33},{49,65},{8... | collective-permute-start | bytes 933896 | tf_op jit(solution)/shard_map/ppermute | solution.py:525
  7.6 1.7 %pack.1 = (f32[2,96,128]{2,1,0:T(8,128)S(1)}, f32[2,96,128]{2,1,0:T(8,128)S(1)}, f32[32,16,256]{2,1,0:T(8,128)S(1)}, f32[32,16,256]{2,1,0:T(8,128)S(1)}) custom-call(s32[5]{0:T(128)S(1)} %stack.23.where_ref, f32[16,64,256]{2,1,0:T(8,128)S(1)} %copy-done, f32[3,64,256]{2,1,0:T(8,128)S(1)} %copy-done.4), custom_call_target="tpu_custom_call" | custom-call | bytes 5250000 | tf_op jit(solution)/shard_map/pack/pallas_call | solution.py:485
  9.3 4.5 %collective-permute-done.1.rows_o.ro_ref = f32[19,16,256]{2,1,0:T(8,128)S(1)} collective-permute-done((f32[19,16,256]{2,1,0:T(8,128)S(1)}, f32[19,16,256]{2,1,0:T(8,128)S(1)}, u32[]{:S(2)}, u32[]{:S(2)}) %collective-permute-start.1) | collective-permute-done | bytes 311328 | tf_op jit(solution)/shard_map/ppermute | solution.py:525
  13.8 0.8 %pack_halo.1 = (f32[2,96,128]{2,1,0:T(8,128)S(1)}, f32[2,96,128]{2,1,0:T(8,128)S(1)}) custom-call(s32[5]{0:T(128)S(1)} %stack.23.where_ref, f32[2,96,128]{2,1,0:T(8,128)S(1)} %get-tuple-element.32.old_e, f32[2,96,128]{2,1,0:T(8,128)S(1)} %get-tuple-element.33.old_o, f32[19,16,256]{2,1,0:T(8,128)S(1)} %collective-permute-done.rows_e.re_ref, ...), custom_call_target="tpu_custom_call" | custom-call | bytes 2450000 | tf_op jit(solution)/shard_map/pack_halo/pallas_call | solution.py:485
  14.6 2.4 %collective-permute-start.4 = (f32[2,96,128]{2,1,0:T(8,128)S(1)}, f32[2,96,128]{2,1,0:T(8,128)S(1)}, u32[]{:S(2)}, u32[]{:S(2)}) collective-permute-start(f32[2,96,128]{2,1,0:T(8,128)S(1)} %get-tuple-element.36), channel_id=1, source_target_pairs={{2,4},{6,8},{10,12},{4,2},{8,6},{12,10},{3,5},{7,9},{11,13},{5,3},... | collective-permute-start | bytes 294920 | tf_op jit(solution)/shard_map/ppermute | solution.py:541
  17.0 2.1 %collective-permute-done.2.peer_ref = f32[16,40,256]{2,1,0:T(8,128)S(1)} collective-permute-done((f32[16,40,256]{2,1,0:T(8,128)S(1)}, f32[16,40,256]{2,1,0:T(8,128)S(1)}, u32[]{:S(2)}, u32[]{:S(2)}) %collective-permute-start.2) | collective-permute-done | bytes 655392 | tf_op jit(solution)/shard_map/ppermute | solution.py:520
  19.2 1.2 %gram.1 = (f32[32,128]{1,0:T(8,128)S(1)}, f32[40,16,256]{2,1,0:T(8,128)S(1)}) custom-call(s32[5]{0:T(128)S(1)} %stack.23.where_ref, f32[32,16,256]{2,1,0:T(8,128)S(1)} %get-tuple-element.37.own_ref.mine_ref, f32[16,40,256]{2,1,0:T(8,128)S(1)} %collective-permute-done.2.peer_ref), custom_call_target="tpu_custom_call" | custom-call | bytes 4200000 | tf_op jit(solution)/shard_map/gram/pallas_call | solution.py:485
  20.4 2.3 %collective-permute-start.3 = (f32[2,96,128]{2,1,0:T(8,128)S(1)}, f32[2,96,128]{2,1,0:T(8,128)S(1)}, u32[]{:S(2)}, u32[]{:S(2)}) collective-permute-start(f32[2,96,128]{2,1,0:T(8,128)S(1)} %get-tuple-element.39), channel_id=1, source_target_pairs={{0,2},{2,0},{4,6},{6,4},{8,10},{10,8},{12,14},{14,12},{1,3},{3,1},... | collective-permute-start | bytes 294920 | tf_op jit(solution)/shard_map/ppermute | solution.py:545
  22.7 1.3 %collective-permute-start.5 = (f32[32,128]{1,0:T(8,128)S(1)}, f32[32,128]{1,0:T(8,128)S(1)}, u32[]{:S(2)}, u32[]{:S(2)}) collective-permute-start(f32[32,128]{1,0:T(8,128)S(1)} %get-tuple-element.43.refs_0_), channel_id=1, source_target_pairs={{0,1},{1,0},{2,3},{3,2},{4,5},{5,4},{6,7},{7,6},{8,9},{9,8},{10,11... | collective-permute-start | bytes 49160 | tf_op jit(solution)/shard_map/ppermute | solution.py:546
  24.0 2.5 %collective-permute-done.5.refs_1_ = f32[32,128]{1,0:T(8,128)S(1)} collective-permute-done((f32[32,128]{1,0:T(8,128)S(1)}, f32[32,128]{1,0:T(8,128)S(1)}, u32[]{:S(2)}, u32[]{:S(2)}) %collective-permute-start.5) | collective-permute-done | bytes 16416 | tf_op jit(solution)/shard_map/ppermute | solution.py:546
  26.4 4.0 %forward.1 = (f32[16,3,80,384]{3,2,1,0:T(8,128)S(1)}, f32[280,256]{1,0:T(8,128)S(1)}) custom-call(s32[5]{0:T(128)S(1)} %stack.23.where_ref, f32[16,64,256]{2,1,0:T(8,128)S(1)} %copy-done.1, f32[19,16,256]{2,1,0:T(8,128)S(1)} %collective-permute-done.rows_e.re_ref, f32[19,16,256]{2,1,0:T(8,128)S(1)} %collective-permute-done.1.rows_o.ro_ref, ...), custom_call_target="tpu_custom_call" | custom-call | bytes 15750000 | tf_op jit(solution)/shard_map/forward/pallas_call | solution.py:485
  30.5 1.4 %collective-permute-start.6 = (f32[280,256]{1,0:T(8,128)S(1)}, f32[280,256]{1,0:T(8,128)S(1)}, u32[]{:S(2)}, u32[]{:S(2)}) collective-permute-start(f32[280,256]{1,0:T(8,128)S(1)} %get-tuple-element.42.t_ref), channel_id=1, source_target_pairs={{0,1},{1,0},{2,3},{3,2},{4,5},{5,4},{6,7},{7,6},{8,9},{9,8},{10,11... | collective-permute-start | bytes 860168 | tf_op jit(solution)/shard_map/ppermute | solution.py:567
  31.9 0.8 %collective-permute-start.7 = (f32[16,16,256]{2,1,0:T(8,128)S(1)}, f32[16,16,256]{2,1,0:T(8,128)S(1)}, u32[]{:S(2)}, u32[]{:S(2)}) collective-permute-start(f32[16,16,256]{2,1,0:T(8,128)S(1)} %slice.6), channel_id=1, source_target_pairs={{0,1},{1,0},{2,3},{3,2},{4,5},{5,4},{6,7},{7,6},{8,9},{9,8},{10,11... | collective-permute-start | bytes 786440 | tf_op jit(solution)/shard_map/ppermute | solution.py:569
  32.7 1.3 %collective-permute-start.8 = (f32[8,16,256]{2,1,0:T(8,128)S(1)}, f32[8,16,256]{2,1,0:T(8,128)S(1)}, u32[]{:S(2)}, u32[]{:S(2)}) collective-permute-start(f32[8,16,256]{2,1,0:T(8,128)S(1)} %slice.7), channel_id=1, source_target_pairs={{0,1},{1,0},{2,3},{3,2},{4,5},{5,4},{6,7},{7,6},{8,9},{9,8},{10,11... | collective-permute-start | bytes 393224 | tf_op jit(solution)/shard_map/ppermute | solution.py:570
  34.0 7.6 %jacobi.1.m_ref = f32[32,128]{1,0:T(8,128)S(1)} custom-call(s32[5]{0:T(128)S(1)} %stack.23.where_ref, f32[32,128]{1,0:T(8,128)S(1)} %get-tuple-element.43.refs_0_, f32[32,128]{1,0:T(8,128)S(1)} %collective-permute-done.5.refs_1_, f32[31,16,128]{2,1,0:T(8,128)S(1)} %copy-done.6), custom_call_target="tpu_custom_call" | custom-call | bytes 29750000 | tf_op jit(solution)/shard_map/jacobi/pallas_call | solution.py:485
  41.6 1.9 %apply_near.1.done_ref = f32[16,64,256]{2,1,0:T(8,128)} custom-call(s32[5]{0:T(128)S(1)} %stack.23.where_ref, f32[32,128]{1,0:T(8,128)S(1)} %jacobi.1.m_ref, f32[32,16,256]{2,1,0:T(8,128)S(1)} %get-tuple-element.37.own_ref.mine_ref, f32[40,16,256]{2,1,0:T(8,128)S(1)} %get-tuple-element.45.near_ref), custom_call_target="tpu_custom_call" | custom-call | bytes 4200000 | tf_op jit(solution)/shard_map/apply_near/pallas_call | solution.py:485
  43.5 3.9 %backward.1 = f32[16,64,256]{2,1,0:T(8,128)} custom-call(s32[5]{0:T(128)S(1)} %stack.23.where_ref, f32[16,3,80,384]{3,2,1,0:T(8,128)S(1)} %get-tuple-element.47.b_ref, f32[280,256]{1,0:T(8,128)S(1)} %get-tuple-element.42.t_ref, f32[280,256]{1,0:T(8,128)S(1)} %collective-permute-done.6.u_ref, f32[3,64,256]{2,1,0:T(8,128)S(1)} %copy-done.5, ...), custom_call_target="tpu_custom_call" | custom-call | bytes 15750000 | tf_op jit(solution)/shard_map/backward/pallas_call | solution.py:485
  47.4 1.9 %apply_far.1 = f32[16,64,256]{2,1,0:T(8,128)} custom-call(s32[5]{0:T(128)S(1)} %stack.23.where_ref, f32[32,128]{1,0:T(8,128)S(1)} %jacobi.1.m_ref, f32[32,16,256]{2,1,0:T(8,128)S(1)} %get-tuple-element.50.other_ref, f32[40,16,256]{2,1,0:T(8,128)S(1)} %get-tuple-element.45.near_ref, ...), custom_call_target="tpu_custom_call", output_to_operand_aliasing={{}: (6, {})} | custom-call | bytes 4200000 | tf_op jit(solution)/shard_map/apply_far/pallas_call | solution.py:485
  (21 shorter events, 0.2 us)
Async XLA Ops:
  0.7 1.2 %copy-start = (f32[16,64,256]{2,1,0:T(8,128)S(1)}, f32[16,64,256]{2,1,0:T(8,128)}, u32[]{:S(2)}) copy-start(f32[16,64,256]{2,1,0:T(8,128)} %x_ref.7) | copy-start | bytes 3145732
  2.6 23.8 %copy-start.1 = (f32[16,64,256]{2,1,0:T(8,128)S(1)}, f32[16,64,256]{2,1,0:T(8,128)}, u32[]{:S(2)}) copy-start(f32[16,64,256]{2,1,0:T(8,128)} %x_ref.7) | copy-start | bytes 3145732
  2.6 23.8 %copy-start.2 = (bf16[3,928,384]{2,1,0:T(8,128)(2,1)S(1)}, bf16[3,928,384]{2,1,0:T(8,128)(2,1)}, u32[]{:S(2)}) copy-start(bf16[3,928,384]{2,1,0:T(8,128)(2,1)} %constant.39.clone.cols_ref.rows_ref) | copy-start | bytes 6414340
  2.6 16.6 %collective-permute-start.2 = (f32[16,40,256]{2,1,0:T(8,128)S(1)}, f32[16,40,256]{2,1,0:T(8,128)S(1)}, u32[]{:S(2)}, u32[]{:S(2)}) collective-permute-start(f32[16,40,256]{2,1,0:T(8,128)S(1)} %cut.1), channel_id=1, source_target_pairs={{0,1},{1,0},{2,3},{3,2},{4,5},{5,4},{6,7},{7,6},{8,9},{9,8},{10,11... | collective-permute-start | bytes 1966088 | tf_op jit(solution)/shard_map/ppermute | solution.py:520
  4.0 0.9 %copy-start.4 = (f32[3,64,256]{2,1,0:T(8,128)S(1)}, f32[3,64,256]{2,1,0:T(8,128)}, u32[]{:S(2)}) copy-start(f32[3,64,256]{2,1,0:T(8,128)} %w_ref.5) | copy-start | bytes 589828
  5.6 8.2 %collective-permute-start.1 = (f32[19,16,256]{2,1,0:T(8,128)S(1)}, f32[19,16,256]{2,1,0:T(8,128)S(1)}, u32[]{:S(2)}, u32[]{:S(2)}) collective-permute-start(f32[19,16,256]{2,1,0:T(8,128)S(1)} %get-tuple-element.30), channel_id=1, source_target_pairs={{16,32},{48,64},{80,96},{32,16},{64,48},{96,80},{17,33},{49,65},{8... | collective-permute-start | bytes 933896 | tf_op jit(solution)/shard_map/ppermute | solution.py:525
  7.5 6.3 %collective-permute-start = (f32[19,16,256]{2,1,0:T(8,128)S(1)}, f32[19,16,256]{2,1,0:T(8,128)S(1)}, u32[]{:S(2)}, u32[]{:S(2)}) collective-permute-start(f32[19,16,256]{2,1,0:T(8,128)S(1)} %get-tuple-element.29), channel_id=1, source_target_pairs={{0,16},{16,0},{32,48},{48,32},{64,80},{80,64},{96,112},{112,96},{1... | collective-permute-start | bytes 933896 | tf_op jit(solution)/shard_map/ppermute | solution.py:526
  14.6 9.4 %collective-permute-start.4 = (f32[2,96,128]{2,1,0:T(8,128)S(1)}, f32[2,96,128]{2,1,0:T(8,128)S(1)}, u32[]{:S(2)}, u32[]{:S(2)}) collective-permute-start(f32[2,96,128]{2,1,0:T(8,128)S(1)} %get-tuple-element.36), channel_id=1, source_target_pairs={{2,4},{6,8},{10,12},{4,2},{8,6},{12,10},{3,5},{7,9},{11,13},{5,3},... | collective-permute-start | bytes 294920 | tf_op jit(solution)/shard_map/ppermute | solution.py:541
  20.4 13.7 %copy-start.6 = (f32[31,16,128]{2,1,0:T(8,128)S(1)}, f32[31,16,128]{2,1,0:T(8,128)}, u32[]{:S(2)}) copy-start(f32[31,16,128]{2,1,0:T(8,128)} %constant.40.clone.refs_2_) | copy-start | bytes 761860
  20.4 6.1 %collective-permute-start.3 = (f32[2,96,128]{2,1,0:T(8,128)S(1)}, f32[2,96,128]{2,1,0:T(8,128)S(1)}, u32[]{:S(2)}, u32[]{:S(2)}) collective-permute-start(f32[2,96,128]{2,1,0:T(8,128)S(1)} %get-tuple-element.39), channel_id=1, source_target_pairs={{0,2},{2,0},{4,6},{6,4},{8,10},{10,8},{12,14},{14,12},{1,3},{3,1},... | collective-permute-start | bytes 294920 | tf_op jit(solution)/shard_map/ppermute | solution.py:545
  22.7 3.7 %collective-permute-start.5 = (f32[32,128]{1,0:T(8,128)S(1)}, f32[32,128]{1,0:T(8,128)S(1)}, u32[]{:S(2)}, u32[]{:S(2)}) collective-permute-start(f32[32,128]{1,0:T(8,128)S(1)} %get-tuple-element.43.refs_0_), channel_id=1, source_target_pairs={{0,1},{1,0},{2,3},{3,2},{4,5},{5,4},{6,7},{7,6},{8,9},{9,8},{10,11... | collective-permute-start | bytes 49160 | tf_op jit(solution)/shard_map/ppermute | solution.py:546
  30.5 13.0 %copy-start.3 = (bf16[3,896,256]{2,1,0:T(8,128)(2,1)S(1)}, bf16[3,896,256]{2,1,0:T(8,128)(2,1)}, u32[]{:S(2)}) copy-start(bf16[3,896,256]{2,1,0:T(8,128)(2,1)} %constant.41.clone.cols_ref.rows_ref) | copy-start | bytes 4128772
  30.5 13.0 %copy-start.5 = (f32[3,64,256]{2,1,0:T(8,128)S(1)}, f32[3,64,256]{2,1,0:T(8,128)}, u32[]{:S(2)}) copy-start(f32[3,64,256]{2,1,0:T(8,128)} %w_ref.5) | copy-start | bytes 589828
  30.5 13.0 %collective-permute-start.6 = (f32[280,256]{1,0:T(8,128)S(1)}, f32[280,256]{1,0:T(8,128)S(1)}, u32[]{:S(2)}, u32[]{:S(2)}) collective-permute-start(f32[280,256]{1,0:T(8,128)S(1)} %get-tuple-element.42.t_ref), channel_id=1, source_target_pairs={{0,1},{1,0},{2,3},{3,2},{4,5},{5,4},{6,7},{7,6},{8,9},{9,8},{10,11... | collective-permute-start | bytes 860168 | tf_op jit(solution)/shard_map/ppermute | solution.py:567
  31.9 15.5 %collective-permute-start.7 = (f32[16,16,256]{2,1,0:T(8,128)S(1)}, f32[16,16,256]{2,1,0:T(8,128)S(1)}, u32[]{:S(2)}, u32[]{:S(2)}) collective-permute-start(f32[16,16,256]{2,1,0:T(8,128)S(1)} %slice.6), channel_id=1, source_target_pairs={{0,1},{1,0},{2,3},{3,2},{4,5},{5,4},{6,7},{7,6},{8,9},{9,8},{10,11... | collective-permute-start | bytes 786440 | tf_op jit(solution)/shard_map/ppermute | solution.py:569
  32.7 14.7 %collective-permute-start.8 = (f32[8,16,256]{2,1,0:T(8,128)S(1)}, f32[8,16,256]{2,1,0:T(8,128)S(1)}, u32[]{:S(2)}, u32[]{:S(2)}) collective-permute-start(f32[8,16,256]{2,1,0:T(8,128)S(1)} %slice.7), channel_id=1, source_target_pairs={{0,1},{1,0},{2,3},{3,2},{4,5},{5,4},{6,7},{7,6},{8,9},{9,8},{10,11... | collective-permute-start | bytes 393224 | tf_op jit(solution)/shard_map/ppermute | solution.py:570

commit v4 on v3

--- a/solution.py
+++ b/solution.py
@@ -26,7 +26,7 @@
 EIN, EOUT = 96, 80
 WIDE = 384
 GRAM_SCALE = float(2.0**32)
-CB = 8
+CB = 16
 
 
 def band_matrix(size, dilation):
@@ -408,7 +408,7 @@
         return table[at, 0:8], table[at, 8:16]
 
     state = lax.fori_loop(
-        0, total // 2, lambda m, held: two_rounds(held, least(2 * m), least(2 * m + 1)), state
+        0, total // 2, lambda m, held: two_rounds(held, least(2 * m), least(2 * m + 1)), state, unroll=2
     )
     if total % 2:
         state = one_round(state, least(total - 1))

time: 49.5 us -> 49.2 us (level)
  no operation moved by 1% of the time
where the time goes in v4:
time: 49.2 us; the launch traced here: 49 us
  Pallas kernels  23.9 us (49%)
  starting transfers between devices  12.9 us (26%)
  waiting for transfers between devices  9.15 us (19%)
  local copies, waits for them, and re-layouts  2.3 us (5%)
  between operations  0.8 us (2%)
    pallas_call x10, Pallas kernels, call(): pl.pallas_call(kernel, out_shape=[jax.ShapeDtypeStruct(s, f32) for s in o...  23.9 us
    ppermute x1, waiting for transfers between devices, shards(): rows_o = lax.ppermute(rim_o, 'frow', odd)  4.53 us
    ppermute x1, waiting for transfers between devices, shards(): got = lax.ppermute(send, 'chan', swap)  2.45 us
    ppermute x1, starting transfers between devices, shards(): cols_o = lax.ppermute(side_o, 'fcol', odd)  2.44 us
    ppermute x1, starting transfers between devices, shards(): cols_e = lax.ppermute(side_e, 'fcol', even)  2.32 us
    unnamed x14, local copies, waits for them, and re-layouts  2.18 us
    ppermute x1, waiting for transfers between devices, shards(): near = lax.ppermute(cut, 'chan', swap)  2.15 us
    ppermute x1, starting transfers between devices, shards(): rows_o = lax.ppermute(rim_o, 'frow', odd)  1.92 us
  transfers between devices with their start and end apart: 9, of which 3 were waited for; matrix products, arithmetic and copies ran while one was open for 0% of the time, Pallas kernels for 36%

profile of v4, /device:TPU:116, one launch (start us, length us, event | category | flops | bytes accessed | tf_op | source)
XLA Modules:
  0.0 49.0 jit_solution(4930602899630766006)
XLA Ops:
  0.7 0.1 stack.23.where_ref
  0.8 1.2 %copy-done = f32[16,64,256]{2,1,0:T(8,128)S(1)} copy-done((f32[16,64,256]{2,1,0:T(8,128)S(1)}, f32[16,64,256]{2,1,0:T(8,128)}, u32[]{:S(2)}) %copy-start) | copy-done | bytes 1048600
  2.0 0.6 %cut.1 = f32[16,40,256]{2,1,0:T(8,128)S(1)} custom-call(s32[5]{0:T(128)S(1)} %stack.23.where_ref, f32[16,64,256]{2,1,0:T(8,128)S(1)} %copy-done), custom_call_target="tpu_custom_call" | custom-call | bytes 2100000 | tf_op jit(solution)/shard_map/cut/pallas_call | solution.py:485
  2.6 1.4 %collective-permute-start.2 = (f32[16,40,256]{2,1,0:T(8,128)S(1)}, f32[16,40,256]{2,1,0:T(8,128)S(1)}, u32[]{:S(2)}, u32[]{:S(2)}) collective-permute-start(f32[16,40,256]{2,1,0:T(8,128)S(1)} %cut.1), channel_id=1, source_target_pairs={{0,1},{1,0},{2,3},{3,2},{4,5},{5,4},{6,7},{7,6},{8,9},{9,8},{10,11... | collective-permute-start | bytes 1966088 | tf_op jit(solution)/shard_map/ppermute | solution.py:520
  4.0 0.9 %copy-done.4 = f32[3,64,256]{2,1,0:T(8,128)S(1)} copy-done((f32[3,64,256]{2,1,0:T(8,128)S(1)}, f32[3,64,256]{2,1,0:T(8,128)}, u32[]{:S(2)}) %copy-start.4) | copy-done | bytes 196632
  4.9 0.7 %rim.1 = (f32[19,16,256]{2,1,0:T(8,128)S(1)}, f32[19,16,256]{2,1,0:T(8,128)S(1)}) custom-call(s32[5]{0:T(128)S(1)} %stack.23.where_ref, f32[16,64,256]{2,1,0:T(8,128)S(1)} %copy-done, f32[3,64,256]{2,1,0:T(8,128)S(1)} %copy-done.4), custom_call_target="tpu_custom_call" | custom-call | bytes 2100000 | tf_op jit(solution)/shard_map/rim/pallas_call | solution.py:485
  5.6 1.9 %collective-permute-start.1 = (f32[19,16,256]{2,1,0:T(8,128)S(1)}, f32[19,16,256]{2,1,0:T(8,128)S(1)}, u32[]{:S(2)}, u32[]{:S(2)}) collective-permute-start(f32[19,16,256]{2,1,0:T(8,128)S(1)} %get-tuple-element.30), channel_id=1, source_target_pairs={{16,32},{48,64},{80,96},{32,16},{64,48},{96,80},{17,33},{49,65},{8... | collective-permute-start | bytes 933896 | tf_op jit(solution)/shard_map/ppermute | solution.py:525
  7.6 1.7 %pack.1 = (f32[2,96,128]{2,1,0:T(8,128)S(1)}, f32[2,96,128]{2,1,0:T(8,128)S(1)}, f32[32,16,256]{2,1,0:T(8,128)S(1)}, f32[32,16,256]{2,1,0:T(8,128)S(1)}) custom-call(s32[5]{0:T(128)S(1)} %stack.23.where_ref, f32[16,64,256]{2,1,0:T(8,128)S(1)} %copy-done, f32[3,64,256]{2,1,0:T(8,128)S(1)} %copy-done.4), custom_call_target="tpu_custom_call" | custom-call | bytes 5250000 | tf_op jit(solution)/shard_map/pack/pallas_call | solution.py:485
  9.3 4.5 %collective-permute-done.1.rows_o.ro_ref = f32[19,16,256]{2,1,0:T(8,128)S(1)} collective-permute-done((f32[19,16,256]{2,1,0:T(8,128)S(1)}, f32[19,16,256]{2,1,0:T(8,128)S(1)}, u32[]{:S(2)}, u32[]{:S(2)}) %collective-permute-start.1) | collective-permute-done | bytes 311328 | tf_op jit(solution)/shard_map/ppermute | solution.py:525
  13.8 0.8 %pack_halo.1 = (f32[2,96,128]{2,1,0:T(8,128)S(1)}, f32[2,96,128]{2,1,0:T(8,128)S(1)}) custom-call(s32[5]{0:T(128)S(1)} %stack.23.where_ref, f32[2,96,128]{2,1,0:T(8,128)S(1)} %get-tuple-element.32.old_e, f32[2,96,128]{2,1,0:T(8,128)S(1)} %get-tuple-element.33.old_o, f32[19,16,256]{2,1,0:T(8,128)S(1)} %collective-permute-done.rows_e.re_ref, ...), custom_call_target="tpu_custom_call" | custom-call | bytes 2450000 | tf_op jit(solution)/shard_map/pack_halo/pallas_call | solution.py:485
  14.6 2.4 %collective-permute-start.4 = (f32[2,96,128]{2,1,0:T(8,128)S(1)}, f32[2,96,128]{2,1,0:T(8,128)S(1)}, u32[]{:S(2)}, u32[]{:S(2)}) collective-permute-start(f32[2,96,128]{2,1,0:T(8,128)S(1)} %get-tuple-element.36), channel_id=1, source_target_pairs={{2,4},{6,8},{10,12},{4,2},{8,6},{12,10},{3,5},{7,9},{11,13},{5,3},... | collective-permute-start | bytes 294920 | tf_op jit(solution)/shard_map/ppermute | solution.py:541
  17.0 2.1 %collective-permute-done.2.peer_ref = f32[16,40,256]{2,1,0:T(8,128)S(1)} collective-permute-done((f32[16,40,256]{2,1,0:T(8,128)S(1)}, f32[16,40,256]{2,1,0:T(8,128)S(1)}, u32[]{:S(2)}, u32[]{:S(2)}) %collective-permute-start.2) | collective-permute-done | bytes 655392 | tf_op jit(solution)/shard_map/ppermute | solution.py:520
  19.2 1.2 %gram.1 = (f32[32,128]{1,0:T(8,128)S(1)}, f32[40,16,256]{2,1,0:T(8,128)S(1)}) custom-call(s32[5]{0:T(128)S(1)} %stack.23.where_ref, f32[32,16,256]{2,1,0:T(8,128)S(1)} %get-tuple-element.37.own_ref.mine_ref, f32[16,40,256]{2,1,0:T(8,128)S(1)} %collective-permute-done.2.peer_ref), custom_call_target="tpu_custom_call" | custom-call | bytes 4200000 | tf_op jit(solution)/shard_map/gram/pallas_call | solution.py:485
  20.4 2.3 %collective-permute-start.3 = (f32[2,96,128]{2,1,0:T(8,128)S(1)}, f32[2,96,128]{2,1,0:T(8,128)S(1)}, u32[]{:S(2)}, u32[]{:S(2)}) collective-permute-start(f32[2,96,128]{2,1,0:T(8,128)S(1)} %get-tuple-element.39), channel_id=1, source_target_pairs={{0,2},{2,0},{4,6},{6,4},{8,10},{10,8},{12,14},{14,12},{1,3},{3,1},... | collective-permute-start | bytes 294920 | tf_op jit(solution)/shard_map/ppermute | solution.py:545
  22.7 1.3 %collective-permute-start.5 = (f32[32,128]{1,0:T(8,128)S(1)}, f32[32,128]{1,0:T(8,128)S(1)}, u32[]{:S(2)}, u32[]{:S(2)}) collective-permute-start(f32[32,128]{1,0:T(8,128)S(1)} %get-tuple-element.43.refs_0_), channel_id=1, source_target_pairs={{0,1},{1,0},{2,3},{3,2},{4,5},{5,4},{6,7},{7,6},{8,9},{9,8},{10,11... | collective-permute-start | bytes 49160 | tf_op jit(solution)/shard_map/ppermute | solution.py:546
  24.0 2.5 %collective-permute-done.5.refs_1_ = f32[32,128]{1,0:T(8,128)S(1)} collective-permute-done((f32[32,128]{1,0:T(8,128)S(1)}, f32[32,128]{1,0:T(8,128)S(1)}, u32[]{:S(2)}, u32[]{:S(2)}) %collective-permute-start.5) | collective-permute-done | bytes 16416 | tf_op jit(solution)/shard_map/ppermute | solution.py:546
  26.4 4.0 %forward.1 = (f32[16,3,80,384]{3,2,1,0:T(8,128)S(1)}, f32[280,256]{1,0:T(8,128)S(1)}) custom-call(s32[5]{0:T(128)S(1)} %stack.23.where_ref, f32[16,64,256]{2,1,0:T(8,128)S(1)} %copy-done.1, f32[19,16,256]{2,1,0:T(8,128)S(1)} %collective-permute-done.rows_e.re_ref, f32[19,16,256]{2,1,0:T(8,128)S(1)} %collective-permute-done.1.rows_o.ro_ref, ...), custom_call_target="tpu_custom_call" | custom-call | bytes 15750000 | tf_op jit(solution)/shard_map/forward/pallas_call | solution.py:485
  30.4 1.4 %collective-permute-start.6 = (f32[280,256]{1,0:T(8,128)S(1)}, f32[280,256]{1,0:T(8,128)S(1)}, u32[]{:S(2)}, u32[]{:S(2)}) collective-permute-start(f32[280,256]{1,0:T(8,128)S(1)} %get-tuple-element.42.t_ref), channel_id=1, source_target_pairs={{0,1},{1,0},{2,3},{3,2},{4,5},{5,4},{6,7},{7,6},{8,9},{9,8},{10,11... | collective-permute-start | bytes 860168 | tf_op jit(solution)/shard_map/ppermute | solution.py:567
  31.8 0.8 %collective-permute-start.7 = (f32[16,16,256]{2,1,0:T(8,128)S(1)}, f32[16,16,256]{2,1,0:T(8,128)S(1)}, u32[]{:S(2)}, u32[]{:S(2)}) collective-permute-start(f32[16,16,256]{2,1,0:T(8,128)S(1)} %slice.6), channel_id=1, source_target_pairs={{0,1},{1,0},{2,3},{3,2},{4,5},{5,4},{6,7},{7,6},{8,9},{9,8},{10,11... | collective-permute-start | bytes 786440 | tf_op jit(solution)/shard_map/ppermute | solution.py:569
  32.6 1.3 %collective-permute-start.8 = (f32[8,16,256]{2,1,0:T(8,128)S(1)}, f32[8,16,256]{2,1,0:T(8,128)S(1)}, u32[]{:S(2)}, u32[]{:S(2)}) collective-permute-start(f32[8,16,256]{2,1,0:T(8,128)S(1)} %slice.7), channel_id=1, source_target_pairs={{0,1},{1,0},{2,3},{3,2},{4,5},{5,4},{6,7},{7,6},{8,9},{9,8},{10,11... | collective-permute-start | bytes 393224 | tf_op jit(solution)/shard_map/ppermute | solution.py:570
  33.9 7.5 %jacobi.1.m_ref = f32[32,128]{1,0:T(8,128)S(1)} custom-call(s32[5]{0:T(128)S(1)} %stack.23.where_ref, f32[32,128]{1,0:T(8,128)S(1)} %get-tuple-element.43.refs_0_, f32[32,128]{1,0:T(8,128)S(1)} %collective-permute-done.5.refs_1_, f32[31,16,128]{2,1,0:T(8,128)S(1)} %copy-done.6), custom_call_target="tpu_custom_call" | custom-call | bytes 29750000 | tf_op jit(solution)/shard_map/jacobi/pallas_call | solution.py:485
  41.4 1.9 %apply_near.1.done_ref = f32[16,64,256]{2,1,0:T(8,128)} custom-call(s32[5]{0:T(128)S(1)} %stack.23.where_ref, f32[32,128]{1,0:T(8,128)S(1)} %jacobi.1.m_ref, f32[32,16,256]{2,1,0:T(8,128)S(1)} %get-tuple-element.37.own_ref.mine_ref, f32[40,16,256]{2,1,0:T(8,128)S(1)} %get-tuple-element.45.near_ref), custom_call_target="tpu_custom_call" | custom-call | bytes 4200000 | tf_op jit(solution)/shard_map/apply_near/pallas_call | solution.py:485
  43.4 3.7 %backward.1 = f32[16,64,256]{2,1,0:T(8,128)} custom-call(s32[5]{0:T(128)S(1)} %stack.23.where_ref, f32[16,3,80,384]{3,2,1,0:T(8,128)S(1)} %get-tuple-element.47.b_ref, f32[280,256]{1,0:T(8,128)S(1)} %get-tuple-element.42.t_ref, f32[280,256]{1,0:T(8,128)S(1)} %collective-permute-done.6.u_ref, f32[3,64,256]{2,1,0:T(8,128)S(1)} %copy-done.5, ...), custom_call_target="tpu_custom_call" | custom-call | bytes 15750000 | tf_op jit(solution)/shard_map/backward/pallas_call | solution.py:485
  47.1 1.9 %apply_far.1 = f32[16,64,256]{2,1,0:T(8,128)} custom-call(s32[5]{0:T(128)S(1)} %stack.23.where_ref, f32[32,128]{1,0:T(8,128)S(1)} %jacobi.1.m_ref, f32[32,16,256]{2,1,0:T(8,128)S(1)} %get-tuple-element.50.other_ref, f32[40,16,256]{2,1,0:T(8,128)S(1)} %get-tuple-element.45.near_ref, ...), custom_call_target="tpu_custom_call", output_to_operand_aliasing={{}: (6, {})} | custom-call | bytes 4200000 | tf_op jit(solution)/shard_map/apply_far/pallas_call | solution.py:485
  (21 shorter events, 0.2 us)
Async XLA Ops:
  0.7 1.2 %copy-start = (f32[16,64,256]{2,1,0:T(8,128)S(1)}, f32[16,64,256]{2,1,0:T(8,128)}, u32[]{:S(2)}) copy-start(f32[16,64,256]{2,1,0:T(8,128)} %x_ref.7) | copy-start | bytes 3145732
  2.6 23.8 %copy-start.1 = (f32[16,64,256]{2,1,0:T(8,128)S(1)}, f32[16,64,256]{2,1,0:T(8,128)}, u32[]{:S(2)}) copy-start(f32[16,64,256]{2,1,0:T(8,128)} %x_ref.7) | copy-start | bytes 3145732
  2.6 23.8 %copy-start.2 = (bf16[3,928,384]{2,1,0:T(8,128)(2,1)S(1)}, bf16[3,928,384]{2,1,0:T(8,128)(2,1)}, u32[]{:S(2)}) copy-start(bf16[3,928,384]{2,1,0:T(8,128)(2,1)} %constant.39.clone.cols_ref.rows_ref) | copy-start | bytes 6414340
  2.6 16.6 %collective-permute-start.2 = (f32[16,40,256]{2,1,0:T(8,128)S(1)}, f32[16,40,256]{2,1,0:T(8,128)S(1)}, u32[]{:S(2)}, u32[]{:S(2)}) collective-permute-start(f32[16,40,256]{2,1,0:T(8,128)S(1)} %cut.1), channel_id=1, source_target_pairs={{0,1},{1,0},{2,3},{3,2},{4,5},{5,4},{6,7},{7,6},{8,9},{9,8},{10,11... | collective-permute-start | bytes 1966088 | tf_op jit(solution)/shard_map/ppermute | solution.py:520
  4.0 0.9 %copy-start.4 = (f32[3,64,256]{2,1,0:T(8,128)S(1)}, f32[3,64,256]{2,1,0:T(8,128)}, u32[]{:S(2)}) copy-start(f32[3,64,256]{2,1,0:T(8,128)} %w_ref.5) | copy-start | bytes 589828
  5.6 8.2 %collective-permute-start.1 = (f32[19,16,256]{2,1,0:T(8,128)S(1)}, f32[19,16,256]{2,1,0:T(8,128)S(1)}, u32[]{:S(2)}, u32[]{:S(2)}) collective-permute-start(f32[19,16,256]{2,1,0:T(8,128)S(1)} %get-tuple-element.30), channel_id=1, source_target_pairs={{16,32},{48,64},{80,96},{32,16},{64,48},{96,80},{17,33},{49,65},{8... | collective-permute-start | bytes 933896 | tf_op jit(solution)/shard_map/ppermute | solution.py:525
  7.5 6.3 %collective-permute-start = (f32[19,16,256]{2,1,0:T(8,128)S(1)}, f32[19,16,256]{2,1,0:T(8,128)S(1)}, u32[]{:S(2)}, u32[]{:S(2)}) collective-permute-start(f32[19,16,256]{2,1,0:T(8,128)S(1)} %get-tuple-element.29), channel_id=1, source_target_pairs={{0,16},{16,0},{32,48},{48,32},{64,80},{80,64},{96,112},{112,96},{1... | collective-permute-start | bytes 933896 | tf_op jit(solution)/shard_map/ppermute | solution.py:526
  14.6 9.4 %collective-permute-start.4 = (f32[2,96,128]{2,1,0:T(8,128)S(1)}, f32[2,96,128]{2,1,0:T(8,128)S(1)}, u32[]{:S(2)}, u32[]{:S(2)}) collective-permute-start(f32[2,96,128]{2,1,0:T(8,128)S(1)} %get-tuple-element.36), channel_id=1, source_target_pairs={{2,4},{6,8},{10,12},{4,2},{8,6},{12,10},{3,5},{7,9},{11,13},{5,3},... | collective-permute-start | bytes 294920 | tf_op jit(solution)/shard_map/ppermute | solution.py:541
  20.4 13.6 %copy-start.6 = (f32[31,16,128]{2,1,0:T(8,128)S(1)}, f32[31,16,128]{2,1,0:T(8,128)}, u32[]{:S(2)}) copy-start(f32[31,16,128]{2,1,0:T(8,128)} %constant.40.clone.refs_2_) | copy-start | bytes 761860
  20.4 6.1 %collective-permute-start.3 = (f32[2,96,128]{2,1,0:T(8,128)S(1)}, f32[2,96,128]{2,1,0:T(8,128)S(1)}, u32[]{:S(2)}, u32[]{:S(2)}) collective-permute-start(f32[2,96,128]{2,1,0:T(8,128)S(1)} %get-tuple-element.39), channel_id=1, source_target_pairs={{0,2},{2,0},{4,6},{6,4},{8,10},{10,8},{12,14},{14,12},{1,3},{3,1},... | collective-permute-start | bytes 294920 | tf_op jit(solution)/shard_map/ppermute | solution.py:545
  22.7 3.7 %collective-permute-start.5 = (f32[32,128]{1,0:T(8,128)S(1)}, f32[32,128]{1,0:T(8,128)S(1)}, u32[]{:S(2)}, u32[]{:S(2)}) collective-permute-start(f32[32,128]{1,0:T(8,128)S(1)} %get-tuple-element.43.refs_0_), channel_id=1, source_target_pairs={{0,1},{1,0},{2,3},{3,2},{4,5},{5,4},{6,7},{7,6},{8,9},{9,8},{10,11... | collective-permute-start | bytes 49160 | tf_op jit(solution)/shard_map/ppermute | solution.py:546
  30.4 13.0 %copy-start.3 = (bf16[3,896,256]{2,1,0:T(8,128)(2,1)S(1)}, bf16[3,896,256]{2,1,0:T(8,128)(2,1)}, u32[]{:S(2)}) copy-start(bf16[3,896,256]{2,1,0:T(8,128)(2,1)} %constant.41.clone.cols_ref.rows_ref) | copy-start | bytes 4128772
  30.4 13.0 %copy-start.5 = (f32[3,64,256]{2,1,0:T(8,128)S(1)}, f32[3,64,256]{2,1,0:T(8,128)}, u32[]{:S(2)}) copy-start(f32[3,64,256]{2,1,0:T(8,128)} %w_ref.5) | copy-start | bytes 589828
  30.4 12.9 %collective-permute-start.6 = (f32[280,256]{1,0:T(8,128)S(1)}, f32[280,256]{1,0:T(8,128)S(1)}, u32[]{:S(2)}, u32[]{:S(2)}) collective-permute-start(f32[280,256]{1,0:T(8,128)S(1)} %get-tuple-element.42.t_ref), channel_id=1, source_target_pairs={{0,1},{1,0},{2,3},{3,2},{4,5},{5,4},{6,7},{7,6},{8,9},{9,8},{10,11... | collective-permute-start | bytes 860168 | tf_op jit(solution)/shard_map/ppermute | solution.py:567
  31.8 15.3 %collective-permute-start.7 = (f32[16,16,256]{2,1,0:T(8,128)S(1)}, f32[16,16,256]{2,1,0:T(8,128)S(1)}, u32[]{:S(2)}, u32[]{:S(2)}) collective-permute-start(f32[16,16,256]{2,1,0:T(8,128)S(1)} %slice.6), channel_id=1, source_target_pairs={{0,1},{1,0},{2,3},{3,2},{4,5},{5,4},{6,7},{7,6},{8,9},{9,8},{10,11... | collective-permute-start | bytes 786440 | tf_op jit(solution)/shard_map/ppermute | solution.py:569
  32.6 14.5 %collective-permute-start.8 = (f32[8,16,256]{2,1,0:T(8,128)S(1)}, f32[8,16,256]{2,1,0:T(8,128)S(1)}, u32[]{:S(2)}, u32[]{:S(2)}) collective-permute-start(f32[8,16,256]{2,1,0:T(8,128)S(1)} %slice.7), channel_id=1, source_target_pairs={{0,1},{1,0},{2,3},{3,2},{4,5},{5,4},{6,7},{7,6},{8,9},{9,8},{10,11... | collective-permute-start | bytes 393224 | tf_op jit(solution)/shard_map/ppermute | solution.py:570
